TPU v7x, 512 devices: a whole 4x8x8 slice. The times are simulated.
512 devices in a mesh: tm: 32 (over y, x_hi, core), head: 16 (over x_lo, z).
Axes of the slice: x: 4 (x_hi: 2, x_lo: 2; x = x_hi * 2 + x_lo), y: 8, z: 8, core: 2. Of those that a mesh axis runs over, the one named last changes fastest.
Arguments:
- queries: bfloat16 [16384, 3072], P(('tm', 'head')), may hold values from -24 to 24
- key_vectors: bfloat16 [16384, 3072], P(('tm', 'head')), may hold values from -24 to 24
- value_vectors: bfloat16 [16384, 3072], P(('tm', 'head')), may hold values from -6 to 6
- frame_order: int32 [64], replicated, may hold values from 0 to 63, each once
- kept_blocks: int32 [64, 12], replicated, may hold values from -1 to 63, as said below
Outputs:
- attended: bfloat16 [16384, 3072], P(('tm', 'head'))
Inputs may be any that keep to these rules, and one draw needn't show every extreme that they name: `kept_blocks`: each row lists distinct frame blocks first and -1 after them; every row lists 4 to 12 blocks, always its own frame block and the frame blocks next to it, and some row lists exactly 12.
All inputs are finite; a program needn't handle non-finite values.
Results may differ from a plain program's by a relative error of at most 0.0085.
Values may be sent and summed in bfloat16 or wider, within the bound.
No kernel may reach another device: no remote copies, remote signals or barrier semaphores. Data moves between devices by JAX's collectives and lax.ppermute only.
A program may use at most 128 MiB of HBM per device.

v0:
```python
import jax
import jax.numpy as jnp
from jax import lax
from jax.sharding import PartitionSpec as P

HD = 64
BLOCK = 256


masked_score = -1e30


def kept_positions(frame_order, kept_rows):
    block_ids = jnp.arange(frame_order.shape[0], dtype=jnp.int32)
    matches = frame_order[None, None, :] == kept_rows[:, :, None]
    positions = jnp.sum(jnp.where(matches, block_ids[None, None, :], 0), axis=2)
    return (positions, kept_rows >= 0)


def attend_block(query_block, key_set, value_set, usable, score_scale):
    scores = (
        jnp.einsum("qhd,jkhd->qhjk", query_block, key_set, preferred_element_type=jnp.float32)
        * score_scale
    )
    live = usable[None, None, :, None]
    scores = jnp.where(live, scores, masked_score)
    best = jnp.max(scores, axis=(2, 3), keepdims=True)
    weights = jnp.where(live, jnp.exp(scores - best), 0.0)
    total = jnp.sum(weights, axis=(2, 3))
    mixed = jnp.einsum(
        "qhjk,jkhd->qhd",
        weights.astype(jnp.bfloat16),
        value_set,
        preferred_element_type=jnp.float32,
    )
    return (mixed / total[:, :, None]).astype(jnp.bfloat16)


def listed_attention(
    query_heads, key_blocks, value_blocks, positions, usable, blocks_here, score_scale
):

    def one_block(which_block):
        query_block = lax.dynamic_slice_in_dim(query_heads, which_block * BLOCK, BLOCK, 0)
        chosen = positions[which_block]
        key_set = jnp.take(key_blocks, chosen, axis=0)
        value_set = jnp.take(value_blocks, chosen, axis=0)
        return attend_block(query_block, key_set, value_set, usable[which_block], score_scale)

    return lax.map(one_block, jnp.arange(blocks_here, dtype=jnp.int32))


def local(queries, key_vectors, value_vectors, frame_order, kept_blocks):
    query_here, keys_here, values_here = (
        lax.all_to_all(queries, "head", split_axis=1, concat_axis=0, tiled=True),
        lax.all_to_all(key_vectors, "head", split_axis=1, concat_axis=0, tiled=True),
        lax.all_to_all(value_vectors, "head", split_axis=1, concat_axis=0, tiled=True),
    )
    row_count = query_here.shape[0]
    feat_width = query_here.shape[1]
    head_count = feat_width // HD
    blocks_here = row_count // BLOCK
    block_total = frame_order.shape[0]
    first_block = lax.axis_index("tm") * blocks_here
    frames = lax.dynamic_slice_in_dim(frame_order, first_block, blocks_here)
    kept_rows = jnp.take(kept_blocks, frames, axis=0)
    positions, usable = kept_positions(frame_order, kept_rows)
    score_scale = HD ** (-0.5)
    query_heads = query_here.reshape(row_count, head_count, HD)
    block_shape = (block_total, BLOCK, head_count, HD)
    whole_keys, whole_values = (
        lax.all_gather(keys_here, "tm", axis=0, tiled=True),
        lax.all_gather(values_here, "tm", axis=0, tiled=True),
    )
    mixed = listed_attention(
        query_heads,
        whole_keys.reshape(block_shape),
        whole_values.reshape(block_shape),
        positions,
        usable,
        blocks_here,
        score_scale,
    )
    merged = mixed.reshape(row_count, feat_width)
    return lax.all_to_all(merged, "head", split_axis=0, concat_axis=1, tiled=True)


def solution(mesh):
    in_specs = (P(("tm", "head"), None), P(("tm", "head"), None), P(("tm", "head"), None), P(), P())
    out_specs = P(("tm", "head"), None)
    return jax.shard_map(local, mesh=mesh, in_specs=in_specs, out_specs=out_specs, check_vma=False)
```

profile of v0, /device:TPU:1, one launch (start us, length us, event | category | flops | bytes accessed | tf_op | source)
XLA Modules:
  0.0 378.5 jit_solution(15524018322816598673)
XLA Ops:
  7.9 20.5 %all_to_all.73 = bf16[32,16,192]{2,0,1:T(8,128)(2,1)} all-to-all(bf16[32,16,192]{2,0,1:T(8,128)(2,1)S(1)} %copy.43), channel_id=1, replica_groups=mesh['tm'=32,'head'=16] {'head'}, dimensions={1} | all-to-all | bytes 393216 | tf_op jit(solution)/shard_map/all_to_all | solution.py:57
  28.5 1.3 all_to_all.58
  29.8 13.1 %all_to_all.74 = bf16[32,16,192]{2,0,1:T(8,128)(2,1)} all-to-all(bf16[32,16,192]{2,0,1:T(8,128)(2,1)S(1)} %copy.45), channel_id=1, replica_groups=mesh['tm'=32,'head'=16] {'head'}, dimensions={1} | all-to-all | bytes 393216 | tf_op jit(solution)/shard_map/all_to_all | solution.py:56
  43.0 1.3 all_to_all.62
  45.1 6.0 %all-to-all-start.2 = ((bf16[32,16,192]{2,0,1:T(8,128)(2,1)}), bf16[32,16,192]{2,0,1:T(8,128)(2,1)S(1)}, u32[]{:S(2)}, u32[]{:S(2)}) async-start(bf16[32,16,192]{2,0,1:T(8,128)(2,1)} %copy.47), calls=%async_computation.2 | async-start | bytes 524288 | tf_op jit(solution)/shard_map/all_to_all | solution.py:55
  54.5 4.4 %all-to-all-done.2 = bf16[32,16,192]{2,0,1:T(8,128)(2,1)S(1)} async-done(((bf16[32,16,192]{2,0,1:T(8,128)(2,1)}), bf16[32,16,192]{2,0,1:T(8,128)(2,1)S(1)}, u32[]{:S(2)}, u32[]{:S(2)}) %all-to-all-start.2) | async-done | bytes 196640 | tf_op jit(solution)/shard_map/all_to_all | solution.py:55
  59.3 76.5 %all-gather.3.cloned.1.call-done = bf16[16384,192]{1,0:T(8,128)(2,1)} async-done(((bf16[512,192]{1,0:T(8,128)(2,1)}), bf16[16384,192]{1,0:T(8,128)(2,1)}) %all-gather.3.cloned.1.call-update) | async-done | bytes 6291472 | tf_op jit(solution)/shard_map/all_gather | solution.py:73
  135.7 30.6 %reshape.91 = bf16[64,256,3,64]{3,2,1,0:T(4,128)(2,1)} reshape(bf16[16384,192]{1,0:T(8,128)(2,1)} %all-gather.3.cloned.1.call-done) | data formatting | bytes 12582912 | tf_op jit(solution)/shard_map/while | solution.py:50
  166.3 76.4 %all-gather.5.cloned.1.call-done = bf16[16384,192]{1,0:T(8,128)(2,1)} async-done(((bf16[512,192]{1,0:T(8,128)(2,1)}), bf16[16384,192]{1,0:T(8,128)(2,1)}) %all-gather.5.cloned.1.call-update) | async-done | bytes 6291472 | tf_op jit(solution)/shard_map/all_gather | solution.py:72
  242.7 30.6 %reshape.92 = bf16[64,256,3,64]{3,2,1,0:T(4,128)(2,1)} reshape(bf16[16384,192]{1,0:T(8,128)(2,1)} %all-gather.5.cloned.1.call-done) | data formatting | bytes 12582912 | tf_op jit(solution)/shard_map/while | solution.py:50
  273.3 80.6 %while.10 = (s32[]{:T(128)}, bf16[2,256,3,64]{1,3,2,0:T(8,128)(2,1)S(1)}, s32[2]{0:T(128)S(1)}, s32[2,12]{1,0:T(2,128)S(1)}, bf16[64,256,3,64]{3,2,1,0:T(4,128)(...) while((s32[]{:T(128)}, ...), condition=%wide.region_4.6_spmd, body=%wide.region_1.0_spmd.sunk | while | flops 635928128 | bytes 47013032 | solution.py:50
  275.6 11.3 %gather_fusion = bf16[12,256,3,64]{3,2,1,0:T(4,128)(2,1)S(1)} fusion(bf16[64,256,3,64]{3,2,1,0:T(4,128)(2,1)} %get-tuple-element.190, s32[1024]{0:T(1024)S(1)} %pad_clamp_fusion.3), kind=kCustom, calls=%fused_computation.clone.clone.1 | custom fusion | bytes 2359344 | tf_op jit(solution)/shard_map/while/body/eval_jaxpr/jit(_take)/gather | solution.py:47
  286.9 10.9 %gather_fusion.1 = bf16[12,256,3,64]{3,2,1,0:T(4,128)(2,1)} fusion(bf16[64,256,3,64]{3,2,1,0:T(4,128)(2,1)} %get-tuple-element.192, s32[1024]{0:T(1024)S(1)} %pad_clamp_fusion.3), kind=kCustom, calls=%fused_computation.1.clone.clone.1 | custom fusion | bytes 2359344 | tf_op jit(solution)/shard_map/while/body/eval_jaxpr/jit(_take)/gather | solution.py:46
  297.7 7.3 %broadcast_select_fusion.5 = (bf16[12,256,3,64]{3,2,1,0:T(4,128)(2,1)}, bf16[12,256,3,64]{3,2,1,0:T(4,128)(2,1)}) fusion(bf16[12,256,3,64]{3,2,1,0:T(4,128)(2,1)S(1)} %gather_fusion, pred[12]{0:T(512)(128)(4,1)S(1)} %get-tuple-element.155, bf16[12,256,3,64]{3,2,1,0:T(4,128)(2,1)} %gather_fusion.1), kind=kLoop, calls=%fused_computation.14.clone.1 | loop fusion | flops 1179648 | bytes 4718604 | tf_op jit(solution)/shard_map/while/body/eval_jaxpr/jit(_take)/select_n | solution.py:47
  305.6 3.4 bitcast_reduce_fusion.2
  309.0 2.4 fusion.50
  311.4 2.2 fusion.51
  315.9 11.3 %gather_fusion = bf16[12,256,3,64]{3,2,1,0:T(4,128)(2,1)S(1)} fusion(bf16[64,256,3,64]{3,2,1,0:T(4,128)(2,1)} %get-tuple-element.190, s32[1024]{0:T(1024)S(1)} %pad_clamp_fusion.3), kind=kCustom, calls=%fused_computation.clone.clone.1 | custom fusion | bytes 2359344 | tf_op jit(solution)/shard_map/while/body/eval_jaxpr/jit(_take)/gather | solution.py:47
  327.2 10.9 %gather_fusion.1 = bf16[12,256,3,64]{3,2,1,0:T(4,128)(2,1)} fusion(bf16[64,256,3,64]{3,2,1,0:T(4,128)(2,1)} %get-tuple-element.192, s32[1024]{0:T(1024)S(1)} %pad_clamp_fusion.3), kind=kCustom, calls=%fused_computation.1.clone.clone.1 | custom fusion | bytes 2359344 | tf_op jit(solution)/shard_map/while/body/eval_jaxpr/jit(_take)/gather | solution.py:46
  338.1 7.3 %broadcast_select_fusion.5 = (bf16[12,256,3,64]{3,2,1,0:T(4,128)(2,1)}, bf16[12,256,3,64]{3,2,1,0:T(4,128)(2,1)}) fusion(bf16[12,256,3,64]{3,2,1,0:T(4,128)(2,1)S(1)} %gather_fusion, pred[12]{0:T(512)(128)(4,1)S(1)} %get-tuple-element.155, bf16[12,256,3,64]{3,2,1,0:T(4,128)(2,1)} %gather_fusion.1), kind=kLoop, calls=%fused_computation.14.clone.1 | loop fusion | flops 1179648 | bytes 4718604 | tf_op jit(solution)/shard_map/while/body/eval_jaxpr/jit(_take)/select_n | solution.py:47
  345.9 3.4 bitcast_reduce_fusion.2
  349.4 2.4 fusion.50
  351.7 2.2 fusion.51
  354.6 16.0 %all_to_all.75 = bf16[16,32,192]{2,1,0:T(8,128)(2,1)S(1)} all-to-all(bf16[16,32,192]{2,1,0:T(8,128)(2,1)S(1)} %all_to_all.65), channel_id=1, replica_groups=mesh['tm'=32,'head'=16] {'head'}, dimensions={0} | all-to-all | bytes 393216 | tf_op jit(solution)/shard_map/all_to_all | solution.py:85
  (44 shorter events, 9.0 us)
Async XLA Ops:
  6.5 129.2 %all-gather.3.cloned.1.call-start = ((), (), s32[]{:S(2)}) async-start(), calls=%async_computation.4 | async-start | bytes 8650752 | tf_op jit(solution)/shard_map/all_gather | solution.py:73
  28.4 214.3 %all-gather.5.cloned.1.call-start = ((), (), s32[]{:S(2)}) async-start(), calls=%async_computation.5 | async-start | bytes 8650752 | tf_op jit(solution)/shard_map/all_gather | solution.py:72
  45.1 13.8 %all-to-all-start.2 = ((bf16[32,16,192]{2,0,1:T(8,128)(2,1)}), bf16[32,16,192]{2,0,1:T(8,128)(2,1)S(1)}, u32[]{:S(2)}, u32[]{:S(2)}) async-start(bf16[32,16,192]{2,0,1:T(8,128)(2,1)} %copy.47), calls=%async_computation.2 | async-start | bytes 524288 | tf_op jit(solution)/shard_map/all_to_all | solution.py:55
  273.3 2.2 copy-start.1
  305.6 5.8 %copy-start = (bf16[12,256,3,64]{3,2,1,0:T(4,128)(2,1)S(1)}, bf16[12,256,3,64]{3,2,1,0:T(4,128)(2,1)}, u32[]{:S(2)}) copy-start(bf16[12,256,3,64]{3,2,1,0:T(4,128)(2,1)} %get-tuple-element.159) | copy-start | bytes 3538948 | tf_op jit(solution)/shard_map/while
  311.4 2.2 copy-start.2
  313.6 2.2 copy-start.1
  345.9 5.8 %copy-start = (bf16[12,256,3,64]{3,2,1,0:T(4,128)(2,1)S(1)}, bf16[12,256,3,64]{3,2,1,0:T(4,128)(2,1)}, u32[]{:S(2)}) copy-start(bf16[12,256,3,64]{3,2,1,0:T(4,128)(2,1)} %get-tuple-element.159) | copy-start | bytes 3538948 | tf_op jit(solution)/shard_map/while
  351.7 2.2 copy-start.2
Sparse Core Ops, SparseCore 0:
  28.6 107.1 all-gather.2
  139.1 103.5 all-gather.4
where the time goes:
time: 381 us; the launch traced here: 379 us
  waiting for transfers between devices  157 us (41%)
  local copies, waits for them, and re-layouts  115 us (30%)
  blocking collectives  49.7 us (13%)
  other arithmetic  21.1 us (6%)
  between operations  13.5 us (4%)
  matrix products  11.2 us (3%)
  starting transfers between devices  6.04 us (2%)
  loops' own time  4.59 us (1%)
    all_gather x1, waiting for transfers between devices, local(): lax.all_gather(values_here, 'tm', axis=0, tiled=True)  76.5 us
    all_gather x1, waiting for transfers between devices, local(): lax.all_gather(keys_here, 'tm', axis=0, tiled=True)  76.4 us
    while x5, local copies, waits for them, and re-layouts, listed_attention(): return lax.map(one_block, jnp.arange(blocks_here, dtype=jnp.int32))  61.8 us
    gather x2, local copies, waits for them, and re-layouts, one_block(): value_set = jnp.take(value_blocks, chosen, axis=0)  22.6 us
    gather x2, local copies, waits for them, and re-layouts, one_block(): key_set = jnp.take(key_blocks, chosen, axis=0)  21.7 us
    all_to_all x1, blocking collectives, local(): lax.all_to_all(value_vectors, 'head', split_axis=1, concat_axis=0, tiled=...  20.5 us
    all_to_all x1, blocking collectives, local(): lax.all_to_all(merged, 'head', split_axis=0, concat_axis=1, tiled=True)  16 us
    select_n x2, other arithmetic, one_block(): value_set = jnp.take(value_blocks, chosen, axis=0)  14.5 us
  transfers between devices with their start and end apart: 3, of which 3 were waited for; matrix products, arithmetic and copies ran while one was open for 9% of the time, Pallas kernels for 0%

commit v1 on v0

v1 whole, which is shorter than its diff:
```python
import jax
import jax.numpy as jnp
from jax import lax
from jax.experimental import pallas as pl
from jax.experimental.pallas import tpu as pltpu
from jax.sharding import PartitionSpec as P

HD = 64
BLOCK = 256
HEADS = 48
NB = 64
KMAX = 12
PAIR = 2 * HD
COLS = 64
SLICE = 32
NY = 8
AXES = ("tm", "head")
MASKED = -1e30
UNROLL = 4
STAGE_SHIFT = 6
STAGE_BASE = 1 << STAGE_SHIFT
LIST = NY * KMAX + UNROLL
EXP2_SCALE = 0.125 * 1.4426950408889634


def flat_index(x, y, z, core):
    return ((y * 2 + (x >> 1)) * 2 + core) * 16 + (x & 1) * 8 + z


COLUMN_GROUPS = [
    [flat_index(x, y, z, c) for y in range(8) for z in range(8)] for x in range(4) for c in range(2)
]


def moves(target):
    return [
        (flat_index(x, y, z, c), flat_index(target(x, c)[0], y, z, target(x, c)[1]))
        for x in range(4)
        for y in range(8)
        for z in range(8)
        for c in range(2)
    ]


SWAP_CORES = moves(lambda x, c: (x, 1 - c))
ONWARD = moves(lambda x, c: ((x + 1 - 2 * c) % 4, c))


def low_lanes(shape):
    return lax.broadcasted_iota(jnp.int32, shape, len(shape) - 1) < HD


def pack_kernel(q_ref, k_ref, v_ref, out_ref):
    low = low_lanes((SLICE, PAIR))
    low_half = low_lanes((SLICE // 2, PAIR))
    half = SLICE // 2
    for pair in range(HEADS // 2):
        lanes = pl.ds(pair * PAIR, PAIR)
        k, v, q = k_ref[:, lanes], v_ref[:, lanes], q_ref[:, lanes]
        k_swap, v_swap, q_swap = (jnp.concatenate([t[:, HD:], t[:, :HD]], axis=1) for t in (k, v, q))
        even, odd = 2 * pair, 2 * pair + 1
        out_ref[even, :SLICE, :] = jnp.where(low, k, v_swap)
        out_ref[odd, :SLICE, :] = jnp.where(low, k_swap, v)
        out_ref[even, SLICE:, :] = jnp.where(low_half, q[:half], q_swap[half:])
        out_ref[odd, SLICE:, :] = jnp.where(low_half, q_swap[:half], q[half:])
    out_ref[HEADS:] = jnp.zeros((COLS - HEADS, SLICE + half, PAIR), jnp.bfloat16)


def unpack_kernel(in_ref, out_ref):
    half = SLICE // 2
    low = low_lanes((half, PAIR))
    for pair in range(HEADS // 2):
        lanes = pl.ds(pair * PAIR, PAIR)
        even, odd = in_ref[2 * pair], in_ref[2 * pair + 1]
        even_swap, odd_swap = (jnp.concatenate([t[:, HD:], t[:, :HD]], axis=1) for t in (even, odd))
        out_ref[:half, lanes] = jnp.where(low, even, odd_swap)
        out_ref[half:, lanes] = jnp.where(low, even_swap, odd)


def list_pairs(order_ref, kept_ref, place_ref, where_is, pairs_ref, counts_ref):
    x_here, core_here, live = place_ref[0], place_ref[1], place_ref[2]

    def place(p, carry):
        away = (((p >> 2) & 1) * 2 + (p & 1) - x_here) & 3
        core = (p >> 1) & 1
        way = (away >> 1) ^ 1
        near = (way ^ core_here) * 2 + (core ^ way)
        part = jnp.where((away & 1) == 1, STAGE_BASE + near * NY, away * STAGE_BASE + (core ^ core_here) * NY)
        where_is[order_ref[p]] = part + (p >> 3)
        return carry

    lax.fori_loop(0, NB, place, 0, unroll=8)

    def list_block(block, ends):
        p = block * NY + (x_here >> 1) * 4 + core_here * 2 + (x_here & 1)
        frame = order_ref[p]
        for j in range(KMAX):
            kept = kept_ref[j, frame]
            there = where_is[jnp.maximum(kept, 0)]
            stage = there >> STAGE_SHIFT
            end = jnp.where(stage == 0, ends[0], jnp.where(stage == 1, ends[1], ends[2]))
            pairs_ref[end] = block * STAGE_BASE + (there & (STAGE_BASE - 1))
            ends = tuple(
                e + ((kept >= 0) & (stage == k)).astype(jnp.int32) for k, e in enumerate(ends)
            )
        return ends

    starts = tuple(stage * LIST for stage in range(3))
    ends = lax.fori_loop(0, NY * live, list_block, tuple(jnp.int32(k) for k in starts))
    for stage in range(3):
        counts_ref[stage] = ends[stage] - starts[stage]
        for u in range(UNROLL):
            pairs_ref[ends[stage] + u] = NY * STAGE_BASE


def spread_queries(mine_ref, q_ref):
    half = SLICE // 2
    for block in range(NY):
        packed = mine_ref[pl.ds(block * NY, NY), SLICE:, :]
        low = low_lanes(packed.shape)
        swapped = jnp.concatenate([packed[:, :, HD:], packed[:, :, :HD]], axis=2)
        zero = jnp.zeros_like(packed)
        q = jnp.concatenate([jnp.where(low, packed, zero), jnp.where(low, swapped, zero)], axis=1)
        q_ref[block] = q.reshape(NY * 2 * half, PAIR)


def add_pairs(stage, pairs_ref, counts_ref, q_ref, kv, best_in, best, mixed_in, mixed, scores, top):
    steps = (counts_ref[stage] + UNROLL - 1) // UNROLL

    def pair(t, u):
        j = t * UNROLL + u
        both = pairs_ref[stage * LIST + j]
        return j, both >> STAGE_SHIFT, both & (STAGE_BASE - 1)

    if best_in is None:
        for block in range(NY + 1):
            top[block] = jnp.full((BLOCK, PAIR), MASKED, jnp.float32)
            mixed[block] = jnp.zeros((BLOCK, PAIR), jnp.float32)
    else:
        for block in range(NY):
            top[block] = best_in[block]

    @pl.loop(0, steps)
    def _(t):
        for u in range(UNROLL):
            j, block, row = pair(t, u)
            s = lax.dot_general(
                q_ref[block], kv[row], (((1,), (1,)), ((), ())), preferred_element_type=jnp.float32
            )
            scores[j] = s
            top[block] = jnp.maximum(top[block], jnp.maximum(s[:, :PAIR], s[:, PAIR:]))

    for block in range(NY):
        new = jnp.broadcast_to(jnp.max(top[block], axis=1, keepdims=True), (BLOCK, PAIR))
        if best_in is not None:
            mixed[block] = mixed_in[block] * jnp.exp2((best_in[block] - new) * EXP2_SCALE)
        best[block] = new

    low = low_lanes((BLOCK, PAIR))

    @pl.loop(0, steps)
    def _(t):
        for u in range(UNROLL):
            j, block, row = pair(t, u)
            peak = best[block]
            s = scores[j]
            weights = jnp.concatenate([s[:, :PAIR] - peak, s[:, PAIR:] - peak], axis=1)
            weights = jnp.exp2(weights * EXP2_SCALE).astype(jnp.bfloat16)
            values = jnp.where(low, jnp.ones((), jnp.bfloat16), kv[row])
            mixed[block] += jnp.dot(weights, values, preferred_element_type=jnp.float32)


def fetch(kv_refs, kv, sems):
    copies = [
        pltpu.make_async_copy(ref, kv.at[pl.ds(i * NY, NY)], sems.at[i]) for i, ref in enumerate(kv_refs)
    ]
    for copy in copies:
        copy.start()
    return copies


def first_kernel(order_ref, kept_ref, place_ref, mine_ref, own_ref, twin_ref, *refs):
    best, mixed, q_ref, pairs_ref, counts_ref, kv, scores, top, where_is, sems = refs
    copies = fetch((own_ref, twin_ref), kv, sems)
    list_pairs(order_ref, kept_ref, place_ref, where_is, pairs_ref, counts_ref)
    spread_queries(mine_ref, q_ref)
    q_ref[NY] = jnp.zeros((BLOCK, PAIR), jnp.bfloat16)
    best[NY] = jnp.zeros((BLOCK, PAIR), jnp.float32)
    for copy in copies:
        copy.wait()
    add_pairs(0, pairs_ref, counts_ref, q_ref, kv, None, best, None, mixed, scores, top)


def second_kernel(pairs_ref, counts_ref, q_ref, best_in, mixed_in, *refs):
    kv_refs = refs[:4]
    best, mixed, kv, scores, top, sems = refs[4:]
    for copy in fetch(kv_refs, kv, sems):
        copy.wait()
    mixed[NY] = jnp.zeros((BLOCK, PAIR), jnp.float32)
    best[NY] = jnp.zeros((BLOCK, PAIR), jnp.float32)
    top[NY] = jnp.zeros((BLOCK, PAIR), jnp.float32)
    add_pairs(1, pairs_ref, counts_ref, q_ref, kv, best_in, best, mixed_in, mixed, scores, top)


def last_kernel(pairs_ref, counts_ref, q_ref, best_in, mixed_in, *refs):
    kv_refs = refs[:2]
    out_ref, best, mixed, kv, scores, top, sems = refs[2:]
    for copy in fetch(kv_refs, kv, sems):
        copy.wait()
    mixed[NY] = jnp.zeros((BLOCK, PAIR), jnp.float32)
    best[NY] = jnp.zeros((BLOCK, PAIR), jnp.float32)
    top[NY] = jnp.zeros((BLOCK, PAIR), jnp.float32)
    add_pairs(2, pairs_ref, counts_ref, q_ref, kv, best_in, best, mixed_in, mixed, scores, top)
    half = SLICE // 2
    low = low_lanes((NY, half, PAIR))
    for block in range(NY):
        both = mixed[block]
        done = both / jnp.concatenate([both[:, HD:], both[:, :HD]], axis=1)
        done = done.reshape(NY, SLICE, PAIR)
        first, second = done[:, :half], done[:, half:]
        first = jnp.concatenate([first[:, :, HD:], first[:, :, :HD]], axis=2)
        out_ref[pl.ds(block * NY, NY)] = jnp.where(low, first, second).astype(jnp.bfloat16)


VMEM = pl.BlockSpec(memory_space=pltpu.VMEM)
SMEM = pl.BlockSpec(memory_space=pltpu.SMEM)
ANY = pl.BlockSpec(memory_space=pl.ANY)


def pack(q, k, v):
    return pl.pallas_call(
        pack_kernel,
        out_shape=jax.ShapeDtypeStruct((COLS, SLICE + SLICE // 2, PAIR), jnp.bfloat16),
        in_specs=[VMEM] * 3,
        out_specs=VMEM,
        name="pack",
    )(q, k, v)


def unpack(mixed):
    return pl.pallas_call(
        unpack_kernel,
        out_shape=jax.ShapeDtypeStruct((SLICE, HEADS * HD), jnp.bfloat16),
        in_specs=[VMEM],
        out_specs=VMEM,
        name="unpack",
    )(mixed)


STATE = jax.ShapeDtypeStruct((NY + 1, BLOCK, PAIR), jnp.float32)


def stage_scratch(chunks):
    return [
        pltpu.VMEM((chunks * NY, BLOCK, PAIR), jnp.bfloat16),
        pltpu.VMEM((NY * KMAX + UNROLL, BLOCK, BLOCK), jnp.float32),
        pltpu.VMEM((NY + 1, BLOCK, PAIR), jnp.float32),
    ]


def stage_options(share):
    return dict(
        compiler_params=pltpu.CompilerParams(vmem_limit_bytes=44 * 1024 * 1024),
        cost_estimate=pl.CostEstimate(flops=share, bytes_accessed=share, transcendentals=share),
    )


def attend_first(order, kept, place, mine, own, twin):
    return pl.pallas_call(
        first_kernel,
        out_shape=(
            STATE,
            STATE,
            jax.ShapeDtypeStruct((NY + 1, BLOCK, PAIR), jnp.bfloat16),
            jax.ShapeDtypeStruct((3 * LIST,), jnp.int32),
            jax.ShapeDtypeStruct((3,), jnp.int32),
        ),
        in_specs=[SMEM] * 3 + [VMEM] + [ANY] * 2,
        out_specs=(VMEM, VMEM, VMEM, SMEM, SMEM),
        scratch_shapes=stage_scratch(2) + [pltpu.SMEM((NB,), jnp.int32), pltpu.SemaphoreType.DMA((2,))],
        name="attend_own",
        **stage_options(1),
    )(order, kept, place, mine, own, twin)


def attend_second(pairs, counts, q, best, mixed, near):
    return pl.pallas_call(
        second_kernel,
        out_shape=(STATE, STATE),
        in_specs=[SMEM] * 2 + [VMEM] * 3 + [ANY] * 4,
        out_specs=(VMEM, VMEM),
        scratch_shapes=stage_scratch(4) + [pltpu.SemaphoreType.DMA((4,))],
        input_output_aliases={3: 0, 4: 1},
        name="attend_near",
        **stage_options(2),
    )(pairs, counts, q, best, mixed, *near)


def attend_last(pairs, counts, q, best, mixed, far):
    return pl.pallas_call(
        last_kernel,
        out_shape=jax.ShapeDtypeStruct((COLS, SLICE // 2, PAIR), jnp.bfloat16),
        in_specs=[SMEM] * 2 + [VMEM] * 3 + [ANY] * 2,
        out_specs=VMEM,
        scratch_shapes=[pltpu.VMEM((NY + 1, BLOCK, PAIR), jnp.float32)] * 2
        + stage_scratch(2)
        + [pltpu.SemaphoreType.DMA((2,))],
        name="attend_far",
        **stage_options(1),
    )(pairs, counts, q, best, mixed, *far)


def local(queries, key_vectors, value_vectors, frame_order, kept_blocks):
    tm, head = lax.axis_index("tm"), lax.axis_index("head")
    x_here = ((tm >> 1) & 1) * 2 + (head >> 3)
    column = (tm >> 2) * 8 + (head & 7)
    place = jnp.stack([x_here, tm & 1, (column < HEADS).astype(jnp.int32)]).astype(jnp.int32)
    packed = pack(queries, key_vectors, value_vectors)
    mine = lax.all_to_all(packed, AXES, 0, 0, tiled=True, axis_index_groups=COLUMN_GROUPS)
    kv = mine[:, :SLICE].reshape(NY, BLOCK, PAIR)
    swap = lambda t: lax.ppermute(t, AXES, SWAP_CORES)
    onward = lambda t: lax.ppermute(t, AXES, ONWARD)
    near_own = onward(kv)
    twin = swap(kv)
    near_twin = onward(twin)
    far = onward(near_own)
    own, twin, near_own = lax.optimization_barrier((kv, twin, near_own))
    best, mixed, q, pairs, counts = attend_first(frame_order, kept_blocks.T, place, mine, own, twin)
    near_own, near_twin, best, mixed = lax.optimization_barrier((near_own, near_twin, best, mixed))
    near = [near_own, near_twin, swap(near_own), swap(near_twin)]
    best, mixed = attend_second(pairs, counts, q, best, mixed, near)
    mixed = attend_last(pairs, counts, q, best, mixed, [far, swap(far)])
    back = lax.all_to_all(mixed, AXES, 0, 0, tiled=True, axis_index_groups=COLUMN_GROUPS)
    return unpack(back)


def solution(mesh):
    tokens = P(AXES, None)
    return jax.shard_map(
        local, mesh=mesh, in_specs=(tokens, tokens, tokens, P(), P()), out_specs=tokens, check_vma=False
    )
```

time: 381 us -> 108 us (0.28)
  waiting for transfers between devices: 157 us -> 3.64 us
  local copies, waits for them, and re-layouts: 115 us -> 0.04 us
  Pallas kernels: 0 us -> 21.5 us
  other arithmetic: 21.1 us -> 0.08 us
  starting transfers between devices: 6.04 us -> 23.4 us
  between operations: 13.5 us -> 0.15 us
  matrix products: 11.2 us -> 0 us
  blocking collectives: 49.7 us -> 58.8 us
  loops' own time: 4.59 us -> 0 us
    all_gather x2 -> x0, waiting for transfers between devices: 153 us -> none  [the longest x1 76.5 us: local(): lax.all_gather(values_here, 'tm', axis=0, tiled=True)]
    while x17 -> x0, local copies, waits for them, and re-layouts: 61.9 us -> none  [the longest x5 61.8 us: listed_attention(): return lax.map(one_block, jnp.arange(blocks_here, dtype=jnp.int32))]
    gather x5 -> x0, local copies, waits for them, and re-layouts: 44.9 us -> none  [the longest x2 22.6 us: one_block(): value_set = jnp.take(value_blocks, chosen, axis=0)]
    ppermute x0 -> x7, starting transfers between devices: none -> 23.4 us  [the longest x3 11.9 us: local(): onward = lambda t: lax.ppermute(t, AXES, ONWARD)]
    pallas_call x0 -> x5, Pallas kernels: none -> 21.5 us  [the longest x1 7.29 us: attend_first(): pl.pallas_call(first_kernel, out_shape=(STATE, STATE, jax.ShapeDtypeStruc...]
    select_n x2 -> x0, other arithmetic: 14.5 us -> none  [one_block(): value_set = jnp.take(value_blocks, chosen, axis=0)]
    dot_general x4 -> x0, matrix products: 11.2 us -> none  [the longest x2 6.85 us: attend_block(): jnp.einsum('qhd,jkhd->qhjk', query_block, key_set, preferred_element_type...]
    all_to_all x3 -> x2, blocking collectives: 49.7 us -> 58.8 us  [the longest x1 38.4 us: local(): lax.all_to_all(packed, AXES, 0, 0, tiled=True, axis_index_groups=COLUMN_G...]
  transfers between devices with their start and end apart: 3 -> 7, of which waited for: 3 -> 1; matrix products, arithmetic and copies ran while one was open for 9% -> 0% of each run, Pallas kernels for 0% -> 12%
where the time goes in v1:
time: 108 us
  blocking collectives  58.8 us (54%)
  starting transfers between devices  23.4 us (22%)
  Pallas kernels  21.5 us (20%)
  waiting for transfers between devices  3.64 us (3%)
    all_to_all x1, blocking collectives, local(): lax.all_to_all(packed, AXES, 0, 0, tiled=True, axis_index_groups=COLUMN_G...  38.4 us
    all_to_all x1, blocking collectives, local(): lax.all_to_all(mixed, AXES, 0, 0, tiled=True, axis_index_groups=COLUMN_GR...  20.4 us
    ppermute x3, starting transfers between devices, local(): onward = lambda t: lax.ppermute(t, AXES, ONWARD)  11.9 us
    ppermute x4, starting transfers between devices, local(): swap = lambda t: lax.ppermute(t, AXES, SWAP_CORES)  11.6 us
    pallas_call x1, Pallas kernels, attend_first(): pl.pallas_call(first_kernel, out_shape=(STATE, STATE, jax.ShapeDtypeStruc...  7.29 us
    pallas_call x1, Pallas kernels, attend_second(): pl.pallas_call(second_kernel, out_shape=(STATE, STATE), in_specs=[SMEM] *...  5.87 us
    pallas_call x1, Pallas kernels, attend_last(): pl.pallas_call(last_kernel, out_shape=jax.ShapeDtypeStruct((COLS, SLICE /...  4.36 us
    ppermute x3, waiting for transfers between devices, local(): onward = lambda t: lax.ppermute(t, AXES, ONWARD)  3.63 us
  transfers between devices with their start and end apart: 7, of which 1 were waited for; matrix products, arithmetic and copies ran while one was open for 0% of the time, Pallas kernels for 12%

profile of v1, /device:TPU:1, one launch (start us, length us, event | category | flops | bytes accessed | tf_op | source)
XLA Modules:
  0.0 107.7 jit_solution(5717911899589441666)
XLA Ops:
  0.0 2.2 %pack.1 = bf16[64,48,128]{2,1,0:T(8,128)(2,1)} custom-call(bf16[32,3072]{1,0:T(8,128)(2,1)} %q_ref.1, bf16[32,3072]{1,0:T(8,128)(2,1)} %k_ref.1, bf16[32,3072]{1,0:T(8,128)(2,1)} %v_ref.1), custom_call_target="tpu_custom_call" | custom-call | tf_op jit(solution)/shard_map/pack/pallas_call | solution.py:231
  2.2 38.4 %all_to_all.10.mine_ref = bf16[64,48,128]{2,1,0:T(8,128)(2,1)S(1)} all-to-all(bf16[64,48,128]{2,1,0:T(8,128)(2,1)} %pack.1), channel_id=1, replica_groups={{0,1,2,3,4,5,6,7,64,65,66,67,68,69,70,71,128,129,130,131,132,133,134,13..., dimensions={0} | all-to-all | bytes 1572864 | tf_op jit(solution)/shard_map/all_to_all | solution.py:319
  40.7 5.3 %collective-permute-start = (bf16[8,256,128]{2,1,0:T(8,128)(2,1)S(1)}, bf16[8,256,128]{2,1,0:T(8,128)(2,1)S(1)}, u32[]{:S(2)}, u32[]{:S(2)}) collective-permute-start(bf16[8,256,128]{2,1,0:T(8,128)(2,1)S(1)} %bitcast.5), channel_id=1, source_target_pairs={{0,16},{16,0},{1,17},{17,1},{2,18},{18,2},{3,19},{19,3},{4,20},{20... | collective-permute-start | bytes 1572872 | tf_op jit(solution)/shard_map/ppermute | solution.py:321
  46.0 4.4 %collective-permute-start.1 = (bf16[8,256,128]{2,1,0:T(8,128)(2,1)S(1)}, bf16[8,256,128]{2,1,0:T(8,128)(2,1)S(1)}, u32[]{:S(2)}, u32[]{:S(2)}) collective-permute-start(bf16[8,256,128]{2,1,0:T(8,128)(2,1)S(1)} %bitcast.6), channel_id=1, source_target_pairs={{0,8},{16,56},{1,9},{17,57},{2,10},{18,58},{3,11},{19,59},{4,12},{... | collective-permute-start | bytes 1572872 | tf_op jit(solution)/shard_map/ppermute | solution.py:322
  50.4 0.0 collective-permute-done.twin_ref
  50.5 2.5 %collective-permute-start.2 = (bf16[8,256,128]{2,1,0:T(8,128)(2,1)S(1)}, bf16[8,256,128]{2,1,0:T(8,128)(2,1)S(1)}, u32[]{:S(2)}, u32[]{:S(2)}) collective-permute-start(bf16[8,256,128]{2,1,0:T(8,128)(2,1)S(1)} %collective-permute-done.twin_ref), channel_id=1, source_target_pairs={{0,8},{16,56},{1,9},{17,57},{2,10},{18,58},{3,11},{19,59},{4,12},{... | collective-permute-start | bytes 1572872 | tf_op jit(solution)/shard_map/ppermute | solution.py:322
  52.9 3.6 %collective-permute-done.1.refs_0_ = bf16[8,256,128]{2,1,0:T(8,128)(2,1)S(1)} collective-permute-done((bf16[8,256,128]{2,1,0:T(8,128)(2,1)S(1)}, bf16[8,256,128]{2,1,0:T(8,128)(2,1)S(1)}, u32[]{:S(2)}, u32[]{:S(2)}) %collective-permute-start.1) | collective-permute-done | bytes 524320 | tf_op jit(solution)/shard_map/ppermute | solution.py:322
  56.5 5.0 %collective-permute-start.5 = (bf16[8,256,128]{2,1,0:T(8,128)(2,1)S(1)}, bf16[8,256,128]{2,1,0:T(8,128)(2,1)S(1)}, u32[]{:S(2)}, u32[]{:S(2)}) collective-permute-start(bf16[8,256,128]{2,1,0:T(8,128)(2,1)S(1)} %collective-permute-done.1.refs_0_), channel_id=1, source_target_pairs={{0,8},{16,56},{1,9},{17,57},{2,10},{18,58},{3,11},{19,59},{4,12},{... | collective-permute-start | bytes 1572872 | tf_op jit(solution)/shard_map/ppermute | solution.py:322
  61.6 0.1 pad_add_fusion.place_ref
  61.7 0.0 copy-done
  61.7 0.0 copy-done.1
  61.7 7.3 %attend_own.1 = (f32[9,256,128]{2,1,0:T(8,128)S(1)}, f32[9,256,128]{2,1,0:T(8,128)S(1)}, bf16[9,256,128]{2,1,0:T(8,128)(2,1)S(1)}, s32[300]{0:T(512)S(1)}, s32[3]{0:T(128)S(1)}) custom-call(s32[64]{0:T(128)S(1)} %copy-done.1, s32[12,64]{1,0:T(8,128)S(1)} %bitcast.8, s32[3]{0:T(128)S(1)} %pad_add_fusion.place_ref, ...), custom_call_target="tpu_custom_call" | custom-call | flops 1 | bytes 1 | tf_op jit(solution)/shard_map/attend_own/pallas_call | solution.py:269
  69.0 0.0 collective-permute-done.2.refs_1_
  69.0 1.9 %collective-permute-start.3 = (bf16[8,256,128]{2,1,0:T(8,128)(2,1)S(1)}, bf16[8,256,128]{2,1,0:T(8,128)(2,1)S(1)}, u32[]{:S(2)}, u32[]{:S(2)}) collective-permute-start(bf16[8,256,128]{2,1,0:T(8,128)(2,1)S(1)} %collective-permute-done.1.refs_0_), channel_id=1, source_target_pairs={{0,16},{16,0},{1,17},{17,1},{2,18},{18,2},{3,19},{19,3},{4,20},{20... | collective-permute-start | bytes 1572872 | tf_op jit(solution)/shard_map/ppermute | solution.py:321
  70.9 2.4 %collective-permute-start.4 = (bf16[8,256,128]{2,1,0:T(8,128)(2,1)S(1)}, bf16[8,256,128]{2,1,0:T(8,128)(2,1)S(1)}, u32[]{:S(2)}, u32[]{:S(2)}) collective-permute-start(bf16[8,256,128]{2,1,0:T(8,128)(2,1)S(1)} %collective-permute-done.2.refs_1_), channel_id=1, source_target_pairs={{0,16},{16,0},{1,17},{17,1},{2,18},{18,2},{3,19},{19,3},{4,20},{20... | collective-permute-start | bytes 1572872 | tf_op jit(solution)/shard_map/ppermute | solution.py:321
  73.3 0.0 collective-permute-done.5.refs_0_
  73.3 1.9 %collective-permute-start.6 = (bf16[8,256,128]{2,1,0:T(8,128)(2,1)S(1)}, bf16[8,256,128]{2,1,0:T(8,128)(2,1)S(1)}, u32[]{:S(2)}, u32[]{:S(2)}) collective-permute-start(bf16[8,256,128]{2,1,0:T(8,128)(2,1)S(1)} %collective-permute-done.5.refs_0_), channel_id=1, source_target_pairs={{0,16},{16,0},{1,17},{17,1},{2,18},{18,2},{3,19},{19,3},{4,20},{20... | collective-permute-start | bytes 1572872 | tf_op jit(solution)/shard_map/ppermute | solution.py:321
  75.2 0.0 collective-permute-done.3.refs_2_
  75.3 0.0 collective-permute-done.4.refs_3_
  75.3 5.9 %attend_near.1 = (f32[9,256,128]{2,1,0:T(8,128)S(1)}, f32[9,256,128]{2,1,0:T(8,128)S(1)}) custom-call(s32[300]{0:T(512)S(1)} %get-tuple-element.21.pairs_ref, s32[3]{0:T(128)S(1)} %get-tuple-element.22.counts_ref, bf16[9,256,128]{2,1,0:T(8,128)(2,1)S(1)} %get-tuple-element.23.q_ref, ...), custom_call_target="tpu_custom_call", output_to_operand_aliasing={{0}: (3, {}), {1}: (4, {})} | custom-call | flops 2 | bytes 2 | tf_op jit(solution)/shard_map/attend_near/pallas_call | solution.py:287
  81.1 0.0 collective-permute-done.6.refs_1_
  81.2 4.4 %attend_far.1 = bf16[64,16,128]{2,1,0:T(8,128)(2,1)S(1)} custom-call(s32[300]{0:T(512)S(1)} %get-tuple-element.21.pairs_ref, s32[3]{0:T(128)S(1)} %get-tuple-element.22.counts_ref, bf16[9,256,128]{2,1,0:T(8,128)(2,1)S(1)} %get-tuple-element.23.q_ref, f32[9,256,128]{2,1,0:T(8,128)S(1)} %get-tuple-element.31.best_in, ...), custom_call_target="tpu_custom_call" | custom-call | flops 1 | bytes 1 | tf_op jit(solution)/shard_map/attend_far/pallas_call | solution.py:300
  85.5 20.4 %all_to_all.11.in_ref = bf16[64,16,128]{2,1,0:T(8,128)(2,1)} all-to-all(bf16[64,16,128]{2,1,0:T(8,128)(2,1)S(1)} %attend_far.1), channel_id=1, replica_groups={{0,1,2,3,4,5,6,7,64,65,66,67,68,69,70,71,128,129,130,131,132,133,134,13..., dimensions={0} | all-to-all | bytes 524288 | tf_op jit(solution)/shard_map/all_to_all | solution.py:333
  105.9 1.7 %unpack.1 = bf16[32,3072]{1,0:T(8,128)(2,1)} custom-call(bf16[64,16,128]{2,1,0:T(8,128)(2,1)} %all_to_all.11.in_ref), custom_call_target="tpu_custom_call" | custom-call | tf_op jit(solution)/shard_map/unpack/pallas_call | solution.py:241
  (3 shorter events, 0.0 us)
Async XLA Ops:
  2.2 59.4 %copy-start = (s32[64,12]{0,1:T(8,128)S(1)}, s32[64,12]{0,1:T(8,128)}, u32[]{:S(2)}) copy-start(s32[64,12]{0,1:T(8,128)} %param.9) | copy-start | bytes 9220
  2.2 59.4 %copy-start.1 = (s32[64]{0:T(128)S(1)}, s32[64]{0:T(128)}, u32[]{:S(2)}) copy-start(s32[64]{0:T(128)} %order_ref.1) | copy-start | bytes 772
  40.7 9.7 %collective-permute-start = (bf16[8,256,128]{2,1,0:T(8,128)(2,1)S(1)}, bf16[8,256,128]{2,1,0:T(8,128)(2,1)S(1)}, u32[]{:S(2)}, u32[]{:S(2)}) collective-permute-start(bf16[8,256,128]{2,1,0:T(8,128)(2,1)S(1)} %bitcast.5), channel_id=1, source_target_pairs={{0,16},{16,0},{1,17},{17,1},{2,18},{18,2},{3,19},{19,3},{4,20},{20... | collective-permute-start | bytes 1572872 | tf_op jit(solution)/shard_map/ppermute | solution.py:321
  46.0 10.5 %collective-permute-start.1 = (bf16[8,256,128]{2,1,0:T(8,128)(2,1)S(1)}, bf16[8,256,128]{2,1,0:T(8,128)(2,1)S(1)}, u32[]{:S(2)}, u32[]{:S(2)}) collective-permute-start(bf16[8,256,128]{2,1,0:T(8,128)(2,1)S(1)} %bitcast.6), channel_id=1, source_target_pairs={{0,8},{16,56},{1,9},{17,57},{2,10},{18,58},{3,11},{19,59},{4,12},{... | collective-permute-start | bytes 1572872 | tf_op jit(solution)/shard_map/ppermute | solution.py:322
  50.5 18.5 %collective-permute-start.2 = (bf16[8,256,128]{2,1,0:T(8,128)(2,1)S(1)}, bf16[8,256,128]{2,1,0:T(8,128)(2,1)S(1)}, u32[]{:S(2)}, u32[]{:S(2)}) collective-permute-start(bf16[8,256,128]{2,1,0:T(8,128)(2,1)S(1)} %collective-permute-done.twin_ref), channel_id=1, source_target_pairs={{0,8},{16,56},{1,9},{17,57},{2,10},{18,58},{3,11},{19,59},{4,12},{... | collective-permute-start | bytes 1572872 | tf_op jit(solution)/shard_map/ppermute | solution.py:322
  56.5 16.8 %collective-permute-start.5 = (bf16[8,256,128]{2,1,0:T(8,128)(2,1)S(1)}, bf16[8,256,128]{2,1,0:T(8,128)(2,1)S(1)}, u32[]{:S(2)}, u32[]{:S(2)}) collective-permute-start(bf16[8,256,128]{2,1,0:T(8,128)(2,1)S(1)} %collective-permute-done.1.refs_0_), channel_id=1, source_target_pairs={{0,8},{16,56},{1,9},{17,57},{2,10},{18,58},{3,11},{19,59},{4,12},{... | collective-permute-start | bytes 1572872 | tf_op jit(solution)/shard_map/ppermute | solution.py:322
  69.0 6.3 %collective-permute-start.3 = (bf16[8,256,128]{2,1,0:T(8,128)(2,1)S(1)}, bf16[8,256,128]{2,1,0:T(8,128)(2,1)S(1)}, u32[]{:S(2)}, u32[]{:S(2)}) collective-permute-start(bf16[8,256,128]{2,1,0:T(8,128)(2,1)S(1)} %collective-permute-done.1.refs_0_), channel_id=1, source_target_pairs={{0,16},{16,0},{1,17},{17,1},{2,18},{18,2},{3,19},{19,3},{4,20},{20... | collective-permute-start | bytes 1572872 | tf_op jit(solution)/shard_map/ppermute | solution.py:321
  70.9 4.4 %collective-permute-start.4 = (bf16[8,256,128]{2,1,0:T(8,128)(2,1)S(1)}, bf16[8,256,128]{2,1,0:T(8,128)(2,1)S(1)}, u32[]{:S(2)}, u32[]{:S(2)}) collective-permute-start(bf16[8,256,128]{2,1,0:T(8,128)(2,1)S(1)} %collective-permute-done.2.refs_1_), channel_id=1, source_target_pairs={{0,16},{16,0},{1,17},{17,1},{2,18},{18,2},{3,19},{19,3},{4,20},{20... | collective-permute-start | bytes 1572872 | tf_op jit(solution)/shard_map/ppermute | solution.py:321
  73.3 7.8 %collective-permute-start.6 = (bf16[8,256,128]{2,1,0:T(8,128)(2,1)S(1)}, bf16[8,256,128]{2,1,0:T(8,128)(2,1)S(1)}, u32[]{:S(2)}, u32[]{:S(2)}) collective-permute-start(bf16[8,256,128]{2,1,0:T(8,128)(2,1)S(1)} %collective-permute-done.5.refs_0_), channel_id=1, source_target_pairs={{0,16},{16,0},{1,17},{17,1},{2,18},{18,2},{3,19},{19,3},{4,20},{20... | collective-permute-start | bytes 1572872 | tf_op jit(solution)/shard_map/ppermute | solution.py:321

commit v2 on v1

v2 whole, which is shorter than its diff:
```python
import jax
import jax.numpy as jnp
from jax import lax
from jax.experimental import pallas as pl
from jax.experimental.pallas import tpu as pltpu
from jax.sharding import PartitionSpec as P

HD = 64
BLOCK = 256
HEADS = 48
NB = 64
KMAX = 12
PAIR = 2 * HD
COLS = 64
SLICE = 32
PARTS = 3
NY = 8
AXES = ("tm", "head")
MASKED = -1e30
UNROLL = 4
QUADS = 4
STAGE_SHIFT = 6
STAGE_BASE = 1 << STAGE_SHIFT
LIST = NY * KMAX + UNROLL
EXP2_SCALE = 0.125 * 1.4426950408889634


def flat_index(x, y, z, core):
    return ((y * 2 + (x >> 1)) * 2 + core) * 16 + (x & 1) * 8 + z


COLUMN_GROUPS = [
    [flat_index(x, y, z, c) for y in range(8) for z in range(8)] for x in range(4) for c in range(2)
]


def moves(target):
    return [
        (flat_index(x, y, z, c), flat_index(target(x, c)[0], y, z, target(x, c)[1]))
        for x in range(4)
        for y in range(8)
        for z in range(8)
        for c in range(2)
    ]


SWAP_CORES = moves(lambda x, c: (x, 1 - c))
ONWARD = moves(lambda x, c: ((x + 1 - 2 * c) % 4, c))
ACROSS = moves(lambda x, c: ((x - 1 + 2 * c) % 4, 1 - c))


def low_lanes(shape):
    return lax.broadcasted_iota(jnp.int32, shape, len(shape) - 1) < HD


def swap_lanes(t):
    return jnp.concatenate([t[:, HD:], t[:, :HD]], axis=1)


def pack_kernel(q_hbm, k_hbm, v_hbm, out_hbm, q_ref, k_ref, v_ref, out_ref, in_sems, out_sems):
    half = SLICE // 2
    low, low_half = low_lanes((SLICE, PAIR)), low_lanes((half, PAIR))
    width, heads = HEADS * HD // PARTS, HEADS // PARTS
    reads, writes = [], []
    for part in range(PARTS):
        lanes = pl.ds(part * width, width)
        reads.append(
            [
                pltpu.make_async_copy(hbm.at[:, lanes], ref.at[:, lanes], in_sems.at[part, i])
                for i, (hbm, ref) in enumerate(((k_hbm, k_ref), (v_hbm, v_ref), (q_hbm, q_ref)))
            ]
        )
        for copy in reads[-1]:
            copy.start()

    def write(first, count):
        columns = pl.ds(first, count)
        copy = pltpu.make_async_copy(out_ref.at[columns], out_hbm.at[columns], out_sems.at[len(writes)])
        copy.start()
        writes.append(copy)

    out_ref[HEADS:] = jnp.zeros((COLS - HEADS, SLICE + half, PAIR), jnp.bfloat16)
    write(HEADS, COLS - HEADS)
    for part in range(PARTS):
        for copy in reads[part]:
            copy.wait()
        for even in range(part * heads, (part + 1) * heads, 2):
            lanes = pl.ds(even * HD, PAIR)
            k, v, q = k_ref[:, lanes], v_ref[:, lanes], q_ref[:, lanes]
            k_swap, v_swap, q_swap = (swap_lanes(t) for t in (k, v, q))
            out_ref[even, :SLICE, :] = jnp.where(low, k, v_swap)
            out_ref[even + 1, :SLICE, :] = jnp.where(low, k_swap, v)
            out_ref[even, SLICE:, :] = jnp.where(low_half, q[:half], q_swap[half:])
            out_ref[even + 1, SLICE:, :] = jnp.where(low_half, q_swap[:half], q[half:])
        write(part * heads, heads)
    for copy in writes:
        copy.wait()


def unpack_kernel(in_ref, out_hbm, out_ref, out_sems):
    half = SLICE // 2
    low = low_lanes((half, PAIR))
    width, heads = HEADS * HD // PARTS, HEADS // PARTS
    writes = []
    for part in range(PARTS):
        for even in range(part * heads, (part + 1) * heads, 2):
            lanes = pl.ds(even * HD, PAIR)
            first, second = in_ref[even], in_ref[even + 1]
            out_ref[:half, lanes] = jnp.where(low, first, swap_lanes(second))
            out_ref[half:, lanes] = jnp.where(low, swap_lanes(first), second)
        lanes = pl.ds(part * width, width)
        copy = pltpu.make_async_copy(out_ref.at[:, lanes], out_hbm.at[:, lanes], out_sems.at[part])
        copy.start()
        writes.append(copy)
    for copy in writes:
        copy.wait()


def list_pairs(order_ref, kept_ref, place_ref, where_is, pairs_ref, counts_ref):
    x_here, core_here, live = place_ref[0], place_ref[1], place_ref[2]

    def place(p, carry):
        away = (((p >> 2) & 1) * 2 + (p & 1) - x_here) & 3
        core = (p >> 1) & 1
        way = (away >> 1) ^ 1
        near = (way ^ core_here) * 2 + (core ^ way)
        near_at = jnp.where(near == 0, 2 * NY, STAGE_BASE + (near - 1) * NY)
        part = jnp.where((away & 1) == 1, near_at, away * STAGE_BASE + (core ^ core_here) * NY)
        where_is[order_ref[p]] = part + (p >> 3)
        return carry

    lax.fori_loop(0, NB, place, 0, unroll=8)

    def list_block(block, ends):
        p = block * NY + (x_here >> 1) * 4 + core_here * 2 + (x_here & 1)
        frame = order_ref[p]
        for j in range(KMAX):
            kept = kept_ref[j, frame]
            there = where_is[jnp.maximum(kept, 0)]
            stage = there >> STAGE_SHIFT
            end = jnp.where(stage == 0, ends[0], jnp.where(stage == 1, ends[1], ends[2]))
            pairs_ref[end] = block * STAGE_BASE + (there & (STAGE_BASE - 1))
            ends = tuple(
                e + ((kept >= 0) & (stage == k)).astype(jnp.int32) for k, e in enumerate(ends)
            )
        return ends

    starts = tuple(stage * LIST for stage in range(3))
    ends = lax.fori_loop(0, NY * live, list_block, tuple(jnp.int32(k) for k in starts))
    for stage in range(3):
        counts_ref[stage] = ends[stage] - starts[stage]
        for u in range(UNROLL):
            pairs_ref[ends[stage] + u] = NY * STAGE_BASE


def spread_queries(mine_ref, q_ref):
    half = SLICE // 2
    for block in range(NY):
        packed = mine_ref[pl.ds(block * NY, NY), SLICE:, :]
        low = low_lanes(packed.shape)
        swapped = jnp.concatenate([packed[:, :, HD:], packed[:, :, :HD]], axis=2)
        zero = jnp.zeros_like(packed)
        q = jnp.concatenate([jnp.where(low, packed, zero), jnp.where(low, swapped, zero)], axis=1)
        q_ref[block] = q.reshape(NY * 2 * half, PAIR)


def add_pairs(stage, pairs_ref, counts_ref, q_ref, kv, best_in, best, mixed_in, mixed, scores, top):
    quads = (counts_ref[stage] + 3) >> 2

    def each_pair(body):
        def run(first, n):
            for u in range(n):
                both = pairs_ref[stage * LIST + first + u]
                body(first + u, both >> STAGE_SHIFT, both & (STAGE_BASE - 1))

        @pl.loop(0, quads // QUADS)
        def _(t):
            run(t * QUADS * 4, QUADS * 4)

        left = quads % QUADS
        for some in range(1, QUADS):

            @pl.when(left == some)
            def _():
                run((quads - some) * 4, some * 4)

    if best_in is None:
        for block in range(NY):
            top[block] = jnp.full((BLOCK, PAIR), MASKED, jnp.float32)
            mixed[block] = jnp.zeros((BLOCK, PAIR), jnp.float32)
    else:
        for block in range(NY):
            top[block] = best_in[block]
    spare = jnp.zeros((BLOCK, PAIR), jnp.float32)
    top[NY], mixed[NY], best[NY] = spare, spare, spare

    def score(j, block, row):
        s = lax.dot_general(q_ref[block], kv[row], (((1,), (1,)), ((), ())), preferred_element_type=jnp.float32)
        scores[j] = s
        top[block] = jnp.maximum(top[block], jnp.maximum(s[:, :PAIR], s[:, PAIR:]))

    each_pair(score)

    for block in range(NY):
        new = jnp.broadcast_to(jnp.max(top[block], axis=1, keepdims=True), (BLOCK, PAIR))
        if best_in is not None:
            mixed[block] = mixed_in[block] * jnp.exp2((best_in[block] - new) * EXP2_SCALE)
        best[block] = new

    low = low_lanes((BLOCK, PAIR))

    def mix(j, block, row):
        peak = best[block]
        s = scores[j]
        weights = jnp.concatenate([s[:, :PAIR] - peak, s[:, PAIR:] - peak], axis=1)
        weights = jnp.exp2(weights * EXP2_SCALE).astype(jnp.bfloat16)
        values = jnp.where(low, jnp.ones((), jnp.bfloat16), kv[row])
        mixed[block] += jnp.dot(weights, values, preferred_element_type=jnp.float32)

    each_pair(mix)


def fetch(kv_refs, kv, sems):
    copies = [
        pltpu.make_async_copy(ref, kv.at[pl.ds(i * NY, NY)], sems.at[i]) for i, ref in enumerate(kv_refs)
    ]
    for copy in copies:
        copy.start()
    return copies


def plan_kernel(order_ref, kept_ref, place_ref, mine_ref, q_ref, pairs_ref, counts_ref, where_is):
    list_pairs(order_ref, kept_ref, place_ref, where_is, pairs_ref, counts_ref)
    spread_queries(mine_ref, q_ref)
    q_ref[NY] = jnp.zeros((BLOCK, PAIR), jnp.bfloat16)


def first_kernel(pairs_ref, counts_ref, q_ref, *refs):
    kv_refs = refs[:3]
    best, mixed, kv, scores, top, sems = refs[3:]
    for copy in fetch(kv_refs, kv, sems):
        copy.wait()
    add_pairs(0, pairs_ref, counts_ref, q_ref, kv, None, best, None, mixed, scores, top)


def second_kernel(pairs_ref, counts_ref, q_ref, best_in, mixed_in, *refs):
    kv_refs = refs[:3]
    best, mixed, kv, scores, top, sems = refs[3:]
    for copy in fetch(kv_refs, kv, sems):
        copy.wait()
    add_pairs(1, pairs_ref, counts_ref, q_ref, kv, best_in, best, mixed_in, mixed, scores, top)


def last_kernel(pairs_ref, counts_ref, q_ref, best_in, mixed_in, *refs):
    kv_refs = refs[:2]
    out_ref, best, mixed, kv, scores, top, sems = refs[2:]
    for copy in fetch(kv_refs, kv, sems):
        copy.wait()
    add_pairs(2, pairs_ref, counts_ref, q_ref, kv, best_in, best, mixed_in, mixed, scores, top)
    half = SLICE // 2
    low = low_lanes((NY, half, PAIR))
    for block in range(NY):
        here = mixed[block]
        there = jnp.concatenate([here[:, HD:], here[:, :HD]], axis=1).reshape(NY, SLICE, PAIR)
        here = here.reshape(NY, SLICE, PAIR)
        values = jnp.where(low, there[:, :half], here[:, half:])
        totals = jnp.where(low, here[:, :half], there[:, half:])
        out_ref[pl.ds(block * NY, NY)] = (values / totals).astype(jnp.bfloat16)


VMEM = pl.BlockSpec(memory_space=pltpu.VMEM)
SMEM = pl.BlockSpec(memory_space=pltpu.SMEM)
ANY = pl.BlockSpec(memory_space=pl.ANY)


def pack(q, k, v):
    rows = pltpu.VMEM((SLICE, HEADS * HD), jnp.bfloat16)
    packed = (COLS, SLICE + SLICE // 2, PAIR)
    return pl.pallas_call(
        pack_kernel,
        out_shape=jax.ShapeDtypeStruct(packed, jnp.bfloat16),
        in_specs=[ANY] * 3,
        out_specs=ANY,
        scratch_shapes=[
            rows,
            rows,
            rows,
            pltpu.VMEM(packed, jnp.bfloat16),
            pltpu.SemaphoreType.DMA((PARTS, 3)),
            pltpu.SemaphoreType.DMA((PARTS + 1,)),
        ],
        name="pack",
    )(q, k, v)


def unpack(mixed):
    return pl.pallas_call(
        unpack_kernel,
        out_shape=jax.ShapeDtypeStruct((SLICE, HEADS * HD), jnp.bfloat16),
        in_specs=[VMEM],
        out_specs=ANY,
        scratch_shapes=[
            pltpu.VMEM((SLICE, HEADS * HD), jnp.bfloat16),
            pltpu.SemaphoreType.DMA((PARTS,)),
        ],
        name="unpack",
    )(mixed)


STATE = jax.ShapeDtypeStruct((NY + 1, BLOCK, PAIR), jnp.float32)


def stage_scratch(chunks):
    return [
        pltpu.VMEM((chunks * NY, BLOCK, PAIR), jnp.bfloat16),
        pltpu.VMEM((NY * KMAX + UNROLL, BLOCK, BLOCK), jnp.float32),
        pltpu.VMEM((NY + 1, BLOCK, PAIR), jnp.float32),
    ]


def stage_options(share):
    return dict(
        compiler_params=pltpu.CompilerParams(vmem_limit_bytes=36 * 1024 * 1024),
        cost_estimate=pl.CostEstimate(flops=share, bytes_accessed=share, transcendentals=share),
    )


def plan(order, kept, place, mine):
    return pl.pallas_call(
        plan_kernel,
        out_shape=(
            jax.ShapeDtypeStruct((NY + 1, BLOCK, PAIR), jnp.bfloat16),
            jax.ShapeDtypeStruct((3 * LIST,), jnp.int32),
            jax.ShapeDtypeStruct((3,), jnp.int32),
        ),
        in_specs=[SMEM] * 3 + [VMEM],
        out_specs=(VMEM, SMEM, SMEM),
        scratch_shapes=[pltpu.SMEM((NB,), jnp.int32)],
        name="plan_pairs",
        **stage_options(1),
    )(order, kept, place, mine)


def attend_first(pairs, counts, q, early):
    return pl.pallas_call(
        first_kernel,
        out_shape=(STATE, STATE),
        in_specs=[SMEM] * 2 + [VMEM] + [ANY] * 3,
        out_specs=(VMEM, VMEM),
        scratch_shapes=stage_scratch(3) + [pltpu.SemaphoreType.DMA((3,))],
        name="attend_early",
        **stage_options(1),
    )(pairs, counts, q, *early)


def attend_second(pairs, counts, q, best, mixed, near):
    return pl.pallas_call(
        second_kernel,
        out_shape=(STATE, STATE),
        in_specs=[SMEM] * 2 + [VMEM] * 3 + [ANY] * 3,
        out_specs=(VMEM, VMEM),
        scratch_shapes=stage_scratch(3) + [pltpu.SemaphoreType.DMA((3,))],
        input_output_aliases={3: 0, 4: 1},
        name="attend_near",
        **stage_options(2),
    )(pairs, counts, q, best, mixed, *near)


def attend_last(pairs, counts, q, best, mixed, far):
    return pl.pallas_call(
        last_kernel,
        out_shape=jax.ShapeDtypeStruct((COLS, SLICE // 2, PAIR), jnp.bfloat16),
        in_specs=[SMEM] * 2 + [VMEM] * 3 + [ANY] * 2,
        out_specs=VMEM,
        scratch_shapes=[pltpu.VMEM((NY + 1, BLOCK, PAIR), jnp.float32)] * 2
        + stage_scratch(2)
        + [pltpu.SemaphoreType.DMA((2,))],
        name="attend_far",
        **stage_options(1),
    )(pairs, counts, q, best, mixed, *far)


def local(queries, key_vectors, value_vectors, frame_order, kept_blocks):
    tm, head = lax.axis_index("tm"), lax.axis_index("head")
    x_here = ((tm >> 1) & 1) * 2 + (head >> 3)
    column = (tm >> 2) * 8 + (head & 7)
    place = jnp.stack([x_here, tm & 1, (column < HEADS).astype(jnp.int32)]).astype(jnp.int32)
    packed = pack(queries, key_vectors, value_vectors)
    mine = lax.all_to_all(packed, AXES, 0, 0, tiled=True, axis_index_groups=COLUMN_GROUPS)
    kv = mine[:, :SLICE].reshape(NY, BLOCK, PAIR)
    swap = lambda t: lax.ppermute(t, AXES, SWAP_CORES)
    onward = lambda t: lax.ppermute(t, AXES, ONWARD)
    near_own = onward(kv)
    twin = swap(kv)
    q, pairs, counts = plan(frame_order, kept_blocks.T, place, mine)
    near_twin = lax.ppermute(kv, AXES, ACROSS)
    near_own, q = lax.optimization_barrier((near_own, q))
    far = onward(near_own)
    best, mixed = attend_first(pairs, counts, q, [kv, twin, near_own])
    near_own, best, mixed = lax.optimization_barrier((near_own, best, mixed))
    near = [near_twin, swap(near_own), swap(near_twin)]
    best, mixed = attend_second(pairs, counts, q, best, mixed, near)
    mixed = attend_last(pairs, counts, q, best, mixed, [far, swap(far)])
    back = lax.all_to_all(mixed, AXES, 0, 0, tiled=True, axis_index_groups=COLUMN_GROUPS)
    return unpack(back)


def solution(mesh):
    tokens = P(AXES, None)
    return jax.shard_map(
        local, mesh=mesh, in_specs=(tokens, tokens, tokens, P(), P()), out_specs=tokens, check_vma=False
    )
```

time: 108 us -> 102 us (0.944)
  waiting for transfers between devices: 3.64 us -> 0.02 us
  Pallas kernels: 21.5 us -> 19.2 us
    ppermute x3 -> x2, starting transfers between devices: 11.9 us -> 7.76 us  [local(): onward = lambda t: lax.ppermute(t, AXES, ONWARD)]
    ppermute x3 -> x2, waiting for transfers between devices: 3.63 us -> 0.01 us  [local(): onward = lambda t: lax.ppermute(t, AXES, ONWARD)]
    ppermute x0 -> x1, starting transfers between devices: none -> 3.01 us  [local(): near_twin = lax.ppermute(kv, AXES, ACROSS)]
    pallas_call x1, Pallas kernels: 5.87 us -> 4.23 us  [attend_second(): pl.pallas_call(second_kernel, out_shape=(STATE, STATE), in_specs=[SMEM] *...]
    pallas_call x2 -> x3, Pallas kernels: 9.5 us -> 9.61 us  [the longest x1 4.55 us: attend_first(): pl.pallas_call(first_kernel, out_shape=(STATE, STATE), in_specs=[SMEM] *...]
  transfers between devices with their start and end apart: 7 -> 7, of which waited for: 1 -> 0; matrix products, arithmetic and copies ran while one was open for 0% -> 0% of each run, Pallas kernels for 12% -> 12%
where the time goes in v2:
time: 102 us; the launch traced here: 101 us
  blocking collectives  58.7 us (58%)
  starting transfers between devices  22.9 us (22%)
  Pallas kernels  19.2 us (19%)
    all_to_all x1, blocking collectives, local(): lax.all_to_all(packed, AXES, 0, 0, tiled=True, axis_index_groups=COLUMN_G...  38.3 us
    all_to_all x1, blocking collectives, local(): lax.all_to_all(mixed, AXES, 0, 0, tiled=True, axis_index_groups=COLUMN_GR...  20.4 us
    ppermute x4, starting transfers between devices, local(): swap = lambda t: lax.ppermute(t, AXES, SWAP_CORES)  12.1 us
    ppermute x2, starting transfers between devices, local(): onward = lambda t: lax.ppermute(t, AXES, ONWARD)  7.76 us
    pallas_call x1, Pallas kernels, attend_first(): pl.pallas_call(first_kernel, out_shape=(STATE, STATE), in_specs=[SMEM] *...  4.55 us
    pallas_call x1, Pallas kernels, attend_second(): pl.pallas_call(second_kernel, out_shape=(STATE, STATE), in_specs=[SMEM] *...  4.23 us
    pallas_call x1, Pallas kernels, attend_last(): pl.pallas_call(last_kernel, out_shape=jax.ShapeDtypeStruct((COLS, SLICE /...  3.64 us
    ppermute x1, starting transfers between devices, local(): near_twin = lax.ppermute(kv, AXES, ACROSS)  3.01 us
  transfers between devices with their start and end apart: 7, of which 0 were waited for; matrix products, arithmetic and copies ran while one was open for 0% of the time, Pallas kernels for 12%

profile of v2, /device:TPU:1, one launch (start us, length us, event | category | flops | bytes accessed | tf_op | source)
XLA Modules:
  0.0 101.3 jit_solution(6138710180564891979)
XLA Ops:
  0.0 2.1 %pack.1 = bf16[64,48,128]{2,1,0:T(8,128)(2,1)} custom-call(bf16[32,3072]{1,0:T(8,128)(2,1)} %q_hbm.1, bf16[32,3072]{1,0:T(8,128)(2,1)} %k_hbm.1, bf16[32,3072]{1,0:T(8,128)(2,1)} %v_hbm.1), custom_call_target="tpu_custom_call" | custom-call | tf_op jit(solution)/shard_map/pack/pallas_call | solution.py:279
  2.1 0.0 copy-start
  2.2 0.0 copy-start.1
  2.2 38.3 %all_to_all.10.mine_ref = bf16[64,48,128]{2,1,0:T(8,128)(2,1)S(1)} all-to-all(bf16[64,48,128]{2,1,0:T(8,128)(2,1)} %pack.1), channel_id=1, replica_groups={{0,1,2,3,4,5,6,7,64,65,66,67,68,69,70,71,128,129,130,131,132,133,134,13..., dimensions={0} | all-to-all | bytes 1572864 | tf_op jit(solution)/shard_map/all_to_all | solution.py:389
  40.5 4.4 %collective-permute-start = (bf16[8,256,128]{2,1,0:T(8,128)(2,1)S(1)}, bf16[8,256,128]{2,1,0:T(8,128)(2,1)S(1)}, u32[]{:S(2)}, u32[]{:S(2)}) collective-permute-start(bf16[8,256,128]{2,1,0:T(8,128)(2,1)S(1)} %bitcast.5), channel_id=1, source_target_pairs={{0,8},{16,56},{1,9},{17,57},{2,10},{18,58},{3,11},{19,59},{4,12},{... | collective-permute-start | bytes 1572872 | tf_op jit(solution)/shard_map/ppermute | solution.py:392
  44.9 4.3 %collective-permute-start.1 = (bf16[8,256,128]{2,1,0:T(8,128)(2,1)S(1)}, bf16[8,256,128]{2,1,0:T(8,128)(2,1)S(1)}, u32[]{:S(2)}, u32[]{:S(2)}) collective-permute-start(bf16[8,256,128]{2,1,0:T(8,128)(2,1)S(1)} %bitcast.6), channel_id=1, source_target_pairs={{0,16},{16,0},{1,17},{17,1},{2,18},{18,2},{3,19},{19,3},{4,20},{20... | collective-permute-start | bytes 1572872 | tf_op jit(solution)/shard_map/ppermute | solution.py:391
  49.3 0.1 pad_add_fusion.place_ref
  49.4 3.0 %collective-permute-start.2 = (bf16[8,256,128]{2,1,0:T(8,128)(2,1)S(1)}, bf16[8,256,128]{2,1,0:T(8,128)(2,1)S(1)}, u32[]{:S(2)}, u32[]{:S(2)}) collective-permute-start(bf16[8,256,128]{2,1,0:T(8,128)(2,1)S(1)} %bitcast.7), channel_id=1, source_target_pairs={{0,56},{16,8},{1,57},{17,9},{2,58},{18,10},{3,59},{19,11},{4,60},{... | collective-permute-start | bytes 1572872 | tf_op jit(solution)/shard_map/ppermute | solution.py:396
  52.4 2.9 %plan_pairs.1 = (bf16[9,256,128]{2,1,0:T(8,128)(2,1)S(1)}, s32[300]{0:T(512)S(1)}, s32[3]{0:T(128)S(1)}) custom-call(s32[64]{0:T(128)S(1)} %copy-done.1, s32[12,64]{1,0:T(8,128)S(1)} %bitcast.9, s32[3]{0:T(128)S(1)} %pad_add_fusion.place_ref, bf16[64,48,128]{2,1,0:T(8,128)(2,1)S(1)} %all_to_all.10.mine_ref), custom_call_target="tpu_custom_call" | custom-call | flops 1 | bytes 1 | tf_op jit(solution)/shard_map/plan_pairs/pallas_call | solution.py:329
  55.3 0.0 collective-permute-done.refs_2_
  55.4 3.4 %collective-permute-start.5 = (bf16[8,256,128]{2,1,0:T(8,128)(2,1)S(1)}, bf16[8,256,128]{2,1,0:T(8,128)(2,1)S(1)}, u32[]{:S(2)}, u32[]{:S(2)}) collective-permute-start(bf16[8,256,128]{2,1,0:T(8,128)(2,1)S(1)} %collective-permute-done.refs_2_), channel_id=1, source_target_pairs={{0,8},{16,56},{1,9},{17,57},{2,10},{18,58},{3,11},{19,59},{4,12},{... | collective-permute-start | bytes 1572872 | tf_op jit(solution)/shard_map/ppermute | solution.py:392
  58.7 0.0 collective-permute-done.1.refs_1_
  58.7 4.5 %attend_early.1 = (f32[9,256,128]{2,1,0:T(8,128)S(1)}, f32[9,256,128]{2,1,0:T(8,128)S(1)}) custom-call(s32[300]{0:T(512)S(1)} %get-tuple-element.17.pairs_ref, s32[3]{0:T(128)S(1)} %get-tuple-element.18.counts_ref, bf16[9,256,128]{2,1,0:T(8,128)(2,1)S(1)} %get-tuple-element.20.q_ref, bf16[8,256,128]{2,1,0:T(8,128)(2,1)S(1)} %bitcast.8, ...), custom_call_target="tpu_custom_call" | custom-call | flops 1 | bytes 1 | tf_op jit(solution)/shard_map/attend_early/pallas_call | solution.py:345
  63.3 2.0 %collective-permute-start.3 = (bf16[8,256,128]{2,1,0:T(8,128)(2,1)S(1)}, bf16[8,256,128]{2,1,0:T(8,128)(2,1)S(1)}, u32[]{:S(2)}, u32[]{:S(2)}) collective-permute-start(bf16[8,256,128]{2,1,0:T(8,128)(2,1)S(1)} %collective-permute-done.refs_2_), channel_id=1, source_target_pairs={{0,16},{16,0},{1,17},{17,1},{2,18},{18,2},{3,19},{19,3},{4,20},{20... | collective-permute-start | bytes 1572872 | tf_op jit(solution)/shard_map/ppermute | solution.py:391
  65.3 0.0 collective-permute-done.2.refs_0_
  65.3 2.4 %collective-permute-start.4 = (bf16[8,256,128]{2,1,0:T(8,128)(2,1)S(1)}, bf16[8,256,128]{2,1,0:T(8,128)(2,1)S(1)}, u32[]{:S(2)}, u32[]{:S(2)}) collective-permute-start(bf16[8,256,128]{2,1,0:T(8,128)(2,1)S(1)} %collective-permute-done.2.refs_0_), channel_id=1, source_target_pairs={{0,16},{16,0},{1,17},{17,1},{2,18},{18,2},{3,19},{19,3},{4,20},{20... | collective-permute-start | bytes 1572872 | tf_op jit(solution)/shard_map/ppermute | solution.py:391
  67.7 0.0 collective-permute-done.5.refs_0_
  67.7 3.5 %collective-permute-start.6 = (bf16[8,256,128]{2,1,0:T(8,128)(2,1)S(1)}, bf16[8,256,128]{2,1,0:T(8,128)(2,1)S(1)}, u32[]{:S(2)}, u32[]{:S(2)}) collective-permute-start(bf16[8,256,128]{2,1,0:T(8,128)(2,1)S(1)} %collective-permute-done.5.refs_0_), channel_id=1, source_target_pairs={{0,16},{16,0},{1,17},{17,1},{2,18},{18,2},{3,19},{19,3},{4,20},{20... | collective-permute-start | bytes 1572872 | tf_op jit(solution)/shard_map/ppermute | solution.py:391
  71.1 0.0 collective-permute-done.3.refs_1_
  71.1 0.0 collective-permute-done.4.refs_2_
  71.2 4.2 %attend_near.1 = (f32[9,256,128]{2,1,0:T(8,128)S(1)}, f32[9,256,128]{2,1,0:T(8,128)S(1)}) custom-call(s32[300]{0:T(512)S(1)} %get-tuple-element.17.pairs_ref, s32[3]{0:T(128)S(1)} %get-tuple-element.18.counts_ref, bf16[9,256,128]{2,1,0:T(8,128)(2,1)S(1)} %get-tuple-element.20.q_ref, ...), custom_call_target="tpu_custom_call", output_to_operand_aliasing={{0}: (3, {}), {1}: (4, {})} | custom-call | flops 2 | bytes 2 | tf_op jit(solution)/shard_map/attend_near/pallas_call | solution.py:357
  75.4 3.6 %attend_far.1 = bf16[64,16,128]{2,1,0:T(8,128)(2,1)S(1)} custom-call(s32[300]{0:T(512)S(1)} %get-tuple-element.17.pairs_ref, s32[3]{0:T(128)S(1)} %get-tuple-element.18.counts_ref, bf16[9,256,128]{2,1,0:T(8,128)(2,1)S(1)} %get-tuple-element.20.q_ref, f32[9,256,128]{2,1,0:T(8,128)S(1)} %get-tuple-element.27.best_in, ...), custom_call_target="tpu_custom_call" | custom-call | flops 1 | bytes 1 | tf_op jit(solution)/shard_map/attend_far/pallas_call | solution.py:370
  79.1 20.4 %all_to_all.11.in_ref = bf16[64,16,128]{2,1,0:T(8,128)(2,1)} all-to-all(bf16[64,16,128]{2,1,0:T(8,128)(2,1)S(1)} %attend_far.1), channel_id=1, replica_groups={{0,1,2,3,4,5,6,7,64,65,66,67,68,69,70,71,128,129,130,131,132,133,134,13..., dimensions={0} | all-to-all | bytes 524288 | tf_op jit(solution)/shard_map/all_to_all | solution.py:404
  99.4 1.7 %unpack.1 = bf16[32,3072]{1,0:T(8,128)(2,1)} custom-call(bf16[64,16,128]{2,1,0:T(8,128)(2,1)} %all_to_all.11.in_ref), custom_call_target="tpu_custom_call" | custom-call | tf_op jit(solution)/shard_map/unpack/pallas_call | solution.py:297
  (4 shorter events, 0.0 us)
Async XLA Ops:
  2.1 50.2 %copy-start = (s32[64,12]{0,1:T(8,128)S(1)}, s32[64,12]{0,1:T(8,128)}, u32[]{:S(2)}) copy-start(s32[64,12]{0,1:T(8,128)} %param.9) | copy-start | bytes 9220
  2.2 50.2 %copy-start.1 = (s32[64]{0:T(128)S(1)}, s32[64]{0:T(128)}, u32[]{:S(2)}) copy-start(s32[64]{0:T(128)} %order_ref.1) | copy-start | bytes 772
  40.5 14.8 %collective-permute-start = (bf16[8,256,128]{2,1,0:T(8,128)(2,1)S(1)}, bf16[8,256,128]{2,1,0:T(8,128)(2,1)S(1)}, u32[]{:S(2)}, u32[]{:S(2)}) collective-permute-start(bf16[8,256,128]{2,1,0:T(8,128)(2,1)S(1)} %bitcast.5), channel_id=1, source_target_pairs={{0,8},{16,56},{1,9},{17,57},{2,10},{18,58},{3,11},{19,59},{4,12},{... | collective-permute-start | bytes 1572872 | tf_op jit(solution)/shard_map/ppermute | solution.py:392
  44.9 13.8 %collective-permute-start.1 = (bf16[8,256,128]{2,1,0:T(8,128)(2,1)S(1)}, bf16[8,256,128]{2,1,0:T(8,128)(2,1)S(1)}, u32[]{:S(2)}, u32[]{:S(2)}) collective-permute-start(bf16[8,256,128]{2,1,0:T(8,128)(2,1)S(1)} %bitcast.6), channel_id=1, source_target_pairs={{0,16},{16,0},{1,17},{17,1},{2,18},{18,2},{3,19},{19,3},{4,20},{20... | collective-permute-start | bytes 1572872 | tf_op jit(solution)/shard_map/ppermute | solution.py:391
  49.4 15.9 %collective-permute-start.2 = (bf16[8,256,128]{2,1,0:T(8,128)(2,1)S(1)}, bf16[8,256,128]{2,1,0:T(8,128)(2,1)S(1)}, u32[]{:S(2)}, u32[]{:S(2)}) collective-permute-start(bf16[8,256,128]{2,1,0:T(8,128)(2,1)S(1)} %bitcast.7), channel_id=1, source_target_pairs={{0,56},{16,8},{1,57},{17,9},{2,58},{18,10},{3,59},{19,11},{4,60},{... | collective-permute-start | bytes 1572872 | tf_op jit(solution)/shard_map/ppermute | solution.py:396
  55.4 12.3 %collective-permute-start.5 = (bf16[8,256,128]{2,1,0:T(8,128)(2,1)S(1)}, bf16[8,256,128]{2,1,0:T(8,128)(2,1)S(1)}, u32[]{:S(2)}, u32[]{:S(2)}) collective-permute-start(bf16[8,256,128]{2,1,0:T(8,128)(2,1)S(1)} %collective-permute-done.refs_2_), channel_id=1, source_target_pairs={{0,8},{16,56},{1,9},{17,57},{2,10},{18,58},{3,11},{19,59},{4,12},{... | collective-permute-start | bytes 1572872 | tf_op jit(solution)/shard_map/ppermute | solution.py:392
  63.3 7.8 %collective-permute-start.3 = (bf16[8,256,128]{2,1,0:T(8,128)(2,1)S(1)}, bf16[8,256,128]{2,1,0:T(8,128)(2,1)S(1)}, u32[]{:S(2)}, u32[]{:S(2)}) collective-permute-start(bf16[8,256,128]{2,1,0:T(8,128)(2,1)S(1)} %collective-permute-done.refs_2_), channel_id=1, source_target_pairs={{0,16},{16,0},{1,17},{17,1},{2,18},{18,2},{3,19},{19,3},{4,20},{20... | collective-permute-start | bytes 1572872 | tf_op jit(solution)/shard_map/ppermute | solution.py:391
  65.3 5.9 %collective-permute-start.4 = (bf16[8,256,128]{2,1,0:T(8,128)(2,1)S(1)}, bf16[8,256,128]{2,1,0:T(8,128)(2,1)S(1)}, u32[]{:S(2)}, u32[]{:S(2)}) collective-permute-start(bf16[8,256,128]{2,1,0:T(8,128)(2,1)S(1)} %collective-permute-done.2.refs_0_), channel_id=1, source_target_pairs={{0,16},{16,0},{1,17},{17,1},{2,18},{18,2},{3,19},{19,3},{4,20},{20... | collective-permute-start | bytes 1572872 | tf_op jit(solution)/shard_map/ppermute | solution.py:391
  67.7 7.7 %collective-permute-start.6 = (bf16[8,256,128]{2,1,0:T(8,128)(2,1)S(1)}, bf16[8,256,128]{2,1,0:T(8,128)(2,1)S(1)}, u32[]{:S(2)}, u32[]{:S(2)}) collective-permute-start(bf16[8,256,128]{2,1,0:T(8,128)(2,1)S(1)} %collective-permute-done.5.refs_0_), channel_id=1, source_target_pairs={{0,16},{16,0},{1,17},{17,1},{2,18},{18,2},{3,19},{19,3},{4,20},{20... | collective-permute-start | bytes 1572872 | tf_op jit(solution)/shard_map/ppermute | solution.py:391

commit v3 on v2

--- a/solution.py
+++ b/solution.py
@@ -57,32 +57,19 @@
     return jnp.concatenate([t[:, HD:], t[:, :HD]], axis=1)
 
 
-def pack_kernel(q_hbm, k_hbm, v_hbm, out_hbm, q_ref, k_ref, v_ref, out_ref, in_sems, out_sems):
+def pack_kernel(q_hbm, k_hbm, v_hbm, out_ref, q_ref, k_ref, v_ref, sems):
     half = SLICE // 2
     low, low_half = low_lanes((SLICE, PAIR)), low_lanes((half, PAIR))
     width, heads = HEADS * HD // PARTS, HEADS // PARTS
-    reads, writes = [], []
+    reads = []
     for part in range(PARTS):
         lanes = pl.ds(part * width, width)
-        reads.append(
-            [
-                pltpu.make_async_copy(hbm.at[:, lanes], ref.at[:, lanes], in_sems.at[part, i])
-                for i, (hbm, ref) in enumerate(((k_hbm, k_ref), (v_hbm, v_ref), (q_hbm, q_ref)))
-            ]
-        )
-        for copy in reads[-1]:
-            copy.start()
-
-    def write(first, count):
-        columns = pl.ds(first, count)
-        copy = pltpu.make_async_copy(out_ref.at[columns], out_hbm.at[columns], out_sems.at[len(writes)])
-        copy.start()
-        writes.append(copy)
-
+        for i, (hbm, ref) in enumerate(((k_hbm, k_ref), (v_hbm, v_ref), (q_hbm, q_ref))):
+            reads.append(pltpu.make_async_copy(hbm.at[:, lanes], ref.at[:, lanes], sems.at[part, i]))
+            reads[-1].start()
     out_ref[HEADS:] = jnp.zeros((COLS - HEADS, SLICE + half, PAIR), jnp.bfloat16)
-    write(HEADS, COLS - HEADS)
     for part in range(PARTS):
-        for copy in reads[part]:
+        for copy in reads[3 * part : 3 * part + 3]:
             copy.wait()
         for even in range(part * heads, (part + 1) * heads, 2):
             lanes = pl.ds(even * HD, PAIR)
@@ -92,9 +79,6 @@
             out_ref[even + 1, :SLICE, :] = jnp.where(low, k_swap, v)
             out_ref[even, SLICE:, :] = jnp.where(low_half, q[:half], q_swap[half:])
             out_ref[even + 1, SLICE:, :] = jnp.where(low_half, q_swap[:half], q[half:])
-        write(part * heads, heads)
-    for copy in writes:
-        copy.wait()
 
 
 def unpack_kernel(in_ref, out_hbm, out_ref, out_sems):
@@ -164,7 +148,7 @@
         q_ref[block] = q.reshape(NY * 2 * half, PAIR)
 
 
-def add_pairs(stage, pairs_ref, counts_ref, q_ref, kv, best_in, best, mixed_in, mixed, scores, top):
+def add_pairs(stage, copies, pairs_ref, counts_ref, q_ref, kv, best_in, best, mixed_in, mixed, scores, top):
     quads = (counts_ref[stage] + 3) >> 2
 
     def each_pair(body):
@@ -193,6 +177,8 @@
             top[block] = best_in[block]
     spare = jnp.zeros((BLOCK, PAIR), jnp.float32)
     top[NY], mixed[NY], best[NY] = spare, spare, spare
+    for copy in copies:
+        copy.wait()
 
     def score(j, block, row):
         s = lax.dot_general(q_ref[block], kv[row], (((1,), (1,)), ((), ())), preferred_element_type=jnp.float32)
@@ -238,25 +224,22 @@
 def first_kernel(pairs_ref, counts_ref, q_ref, *refs):
     kv_refs = refs[:3]
     best, mixed, kv, scores, top, sems = refs[3:]
-    for copy in fetch(kv_refs, kv, sems):
-        copy.wait()
-    add_pairs(0, pairs_ref, counts_ref, q_ref, kv, None, best, None, mixed, scores, top)
+    copies = fetch(kv_refs, kv, sems)
+    add_pairs(0, copies, pairs_ref, counts_ref, q_ref, kv, None, best, None, mixed, scores, top)
 
 
 def second_kernel(pairs_ref, counts_ref, q_ref, best_in, mixed_in, *refs):
     kv_refs = refs[:3]
     best, mixed, kv, scores, top, sems = refs[3:]
-    for copy in fetch(kv_refs, kv, sems):
-        copy.wait()
-    add_pairs(1, pairs_ref, counts_ref, q_ref, kv, best_in, best, mixed_in, mixed, scores, top)
+    copies = fetch(kv_refs, kv, sems)
+    add_pairs(1, copies, pairs_ref, counts_ref, q_ref, kv, best_in, best, mixed_in, mixed, scores, top)
 
 
 def last_kernel(pairs_ref, counts_ref, q_ref, best_in, mixed_in, *refs):
     kv_refs = refs[:2]
     out_ref, best, mixed, kv, scores, top, sems = refs[2:]
-    for copy in fetch(kv_refs, kv, sems):
-        copy.wait()
-    add_pairs(2, pairs_ref, counts_ref, q_ref, kv, best_in, best, mixed_in, mixed, scores, top)
+    copies = fetch(kv_refs, kv, sems)
+    add_pairs(2, copies, pairs_ref, counts_ref, q_ref, kv, best_in, best, mixed_in, mixed, scores, top)
     half = SLICE // 2
     low = low_lanes((NY, half, PAIR))
     for block in range(NY):
@@ -275,20 +258,12 @@
 
 def pack(q, k, v):
     rows = pltpu.VMEM((SLICE, HEADS * HD), jnp.bfloat16)
-    packed = (COLS, SLICE + SLICE // 2, PAIR)
     return pl.pallas_call(
         pack_kernel,
-        out_shape=jax.ShapeDtypeStruct(packed, jnp.bfloat16),
+        out_shape=pltpu.VMEM((COLS, SLICE + SLICE // 2, PAIR), jnp.bfloat16),
         in_specs=[ANY] * 3,
-        out_specs=ANY,
-        scratch_shapes=[
-            rows,
-            rows,
-            rows,
-            pltpu.VMEM(packed, jnp.bfloat16),
-            pltpu.SemaphoreType.DMA((PARTS, 3)),
-            pltpu.SemaphoreType.DMA((PARTS + 1,)),
-        ],
+        out_specs=VMEM,
+        scratch_shapes=[rows, rows, rows, pltpu.SemaphoreType.DMA((PARTS, 3))],
         name="pack",
     )(q, k, v)
 
@@ -330,8 +305,8 @@
         plan_kernel,
         out_shape=(
             jax.ShapeDtypeStruct((NY + 1, BLOCK, PAIR), jnp.bfloat16),
-            jax.ShapeDtypeStruct((3 * LIST,), jnp.int32),
-            jax.ShapeDtypeStruct((3,), jnp.int32),
+            pltpu.SMEM((3 * LIST,), jnp.int32),
+            pltpu.SMEM((3,), jnp.int32),
         ),
         in_specs=[SMEM] * 3 + [VMEM],
         out_specs=(VMEM, SMEM, SMEM),
@@ -402,7 +377,7 @@
     best, mixed = attend_second(pairs, counts, q, best, mixed, near)
     mixed = attend_last(pairs, counts, q, best, mixed, [far, swap(far)])
     back = lax.all_to_all(mixed, AXES, 0, 0, tiled=True, axis_index_groups=COLUMN_GROUPS)
-    return unpack(back)
+    return unpack(pltpu.with_memory_space_constraint(back, pltpu.VMEM))
 
 
 def solution(mesh):

time: 102 us -> 97 us (0.951); the launches traced: 101 us -> 95.2 us
  Pallas kernels: 19.2 us -> 14 us
  blocking collectives: 58.7 us -> 57.1 us
    pallas_call x1, Pallas kernels: 4.23 us -> 2.59 us  [attend_second(): pl.pallas_call(second_kernel, out_shape=(STATE, STATE), in_specs=[SMEM] *...]
    all_to_all x1, blocking collectives: 20.4 us -> 19 us  [local(): lax.all_to_all(mixed, AXES, 0, 0, tiled=True, axis_index_groups=COLUMN_GR...]
    pallas_call x1, Pallas kernels: 3.64 us -> 2.47 us  [attend_last(): pl.pallas_call(last_kernel, out_shape=jax.ShapeDtypeStruct((COLS, SLICE /...]
  transfers between devices with their start and end apart: 7 -> 7, of which waited for: 0 -> 0; matrix products, arithmetic and copies ran while one was open for 0% -> 0% of each run, Pallas kernels for 12% -> 10%
where the time goes in v3:
time: 97 us; the launch traced here: 95.2 us
  blocking collectives  57.1 us (59%)
  starting transfers between devices  23.6 us (24%)
  Pallas kernels  14 us (14%)
    all_to_all x1, blocking collectives, local(): lax.all_to_all(packed, AXES, 0, 0, tiled=True, axis_index_groups=COLUMN_G...  38.1 us
    all_to_all x1, blocking collectives, local(): lax.all_to_all(mixed, AXES, 0, 0, tiled=True, axis_index_groups=COLUMN_GR...  19 us
    ppermute x4, starting transfers between devices, local(): swap = lambda t: lax.ppermute(t, AXES, SWAP_CORES)  12.8 us
    ppermute x2, starting transfers between devices, local(): onward = lambda t: lax.ppermute(t, AXES, ONWARD)  7.76 us
    pallas_call x1, Pallas kernels, attend_first(): pl.pallas_call(first_kernel, out_shape=(STATE, STATE), in_specs=[SMEM] *...  4.41 us
    ppermute x1, starting transfers between devices, local(): near_twin = lax.ppermute(kv, AXES, ACROSS)  3.01 us
    pallas_call x1, Pallas kernels, attend_second(): pl.pallas_call(second_kernel, out_shape=(STATE, STATE), in_specs=[SMEM] *...  2.59 us
    pallas_call x1, Pallas kernels, attend_last(): pl.pallas_call(last_kernel, out_shape=jax.ShapeDtypeStruct((COLS, SLICE /...  2.47 us
  transfers between devices with their start and end apart: 7, of which 0 were waited for; matrix products, arithmetic and copies ran while one was open for 0% of the time, Pallas kernels for 10%

profile of v3, /device:TPU:1, one launch (start us, length us, event | category | flops | bytes accessed | tf_op | source)
XLA Modules:
  0.0 95.2 jit_solution(12126878193266629637)
XLA Ops:
  0.0 1.4 %pack.1 = bf16[64,48,128]{2,1,0:T(8,128)(2,1)S(1)} custom-call(bf16[32,3072]{1,0:T(8,128)(2,1)} %q_hbm.1, bf16[32,3072]{1,0:T(8,128)(2,1)} %k_hbm.1, bf16[32,3072]{1,0:T(8,128)(2,1)} %v_hbm.1), custom_call_target="tpu_custom_call" | custom-call | tf_op jit(solution)/shard_map/pack/pallas_call | solution.py:261
  1.4 0.0 copy-start
  1.4 0.0 copy-start.1
  1.4 38.1 %all_to_all.10.mine_ref = bf16[64,48,128]{2,1,0:T(8,128)(2,1)S(1)} all-to-all(bf16[64,48,128]{2,1,0:T(8,128)(2,1)S(1)} %pack.1), channel_id=1, replica_groups={{0,1,2,3,4,5,6,7,64,65,66,67,68,69,70,71,128,129,130,131,132,133,134,13..., dimensions={0} | all-to-all | bytes 1572864 | tf_op jit(solution)/shard_map/all_to_all | solution.py:364
  39.6 4.4 %collective-permute-start = (bf16[8,256,128]{2,1,0:T(8,128)(2,1)S(1)}, bf16[8,256,128]{2,1,0:T(8,128)(2,1)S(1)}, u32[]{:S(2)}, u32[]{:S(2)}) collective-permute-start(bf16[8,256,128]{2,1,0:T(8,128)(2,1)S(1)} %bitcast.5), channel_id=1, source_target_pairs={{0,8},{16,56},{1,9},{17,57},{2,10},{18,58},{3,11},{19,59},{4,12},{... | collective-permute-start | bytes 1572872 | tf_op jit(solution)/shard_map/ppermute | solution.py:367
  44.0 4.3 %collective-permute-start.1 = (bf16[8,256,128]{2,1,0:T(8,128)(2,1)S(1)}, bf16[8,256,128]{2,1,0:T(8,128)(2,1)S(1)}, u32[]{:S(2)}, u32[]{:S(2)}) collective-permute-start(bf16[8,256,128]{2,1,0:T(8,128)(2,1)S(1)} %bitcast.6), channel_id=1, source_target_pairs={{0,16},{16,0},{1,17},{17,1},{2,18},{18,2},{3,19},{19,3},{4,20},{20... | collective-permute-start | bytes 1572872 | tf_op jit(solution)/shard_map/ppermute | solution.py:366
  48.3 0.1 pad_add_fusion.place_ref
  48.4 3.0 %collective-permute-start.2 = (bf16[8,256,128]{2,1,0:T(8,128)(2,1)S(1)}, bf16[8,256,128]{2,1,0:T(8,128)(2,1)S(1)}, u32[]{:S(2)}, u32[]{:S(2)}) collective-permute-start(bf16[8,256,128]{2,1,0:T(8,128)(2,1)S(1)} %bitcast.7), channel_id=1, source_target_pairs={{0,56},{16,8},{1,57},{17,9},{2,58},{18,10},{3,59},{19,11},{4,60},{... | collective-permute-start | bytes 1572872 | tf_op jit(solution)/shard_map/ppermute | solution.py:371
  51.4 2.4 %plan_pairs.1 = (bf16[9,256,128]{2,1,0:T(8,128)(2,1)S(1)}, s32[300]{0:T(512)S(4)}, s32[3]{0:T(128)S(4)}) custom-call(s32[64]{0:T(128)S(1)} %copy-done.1, s32[12,64]{1,0:T(8,128)S(1)} %bitcast.9, s32[3]{0:T(128)S(1)} %pad_add_fusion.place_ref, bf16[64,48,128]{2,1,0:T(8,128)(2,1)S(1)} %all_to_all.10.mine_ref), custom_call_target="tpu_custom_call" | custom-call | flops 1 | bytes 1 | tf_op jit(solution)/shard_map/plan_pairs/pallas_call | solution.py:304
  53.8 0.0 collective-permute-done.refs_2_
  53.8 3.4 %collective-permute-start.5 = (bf16[8,256,128]{2,1,0:T(8,128)(2,1)S(1)}, bf16[8,256,128]{2,1,0:T(8,128)(2,1)S(1)}, u32[]{:S(2)}, u32[]{:S(2)}) collective-permute-start(bf16[8,256,128]{2,1,0:T(8,128)(2,1)S(1)} %collective-permute-done.refs_2_), channel_id=1, source_target_pairs={{0,8},{16,56},{1,9},{17,57},{2,10},{18,58},{3,11},{19,59},{4,12},{... | collective-permute-start | bytes 1572872 | tf_op jit(solution)/shard_map/ppermute | solution.py:367
  57.2 0.0 collective-permute-done.1.refs_1_
  57.2 4.4 %attend_early.1 = (f32[9,256,128]{2,1,0:T(8,128)S(1)}, f32[9,256,128]{2,1,0:T(8,128)S(1)}) custom-call(s32[300]{0:T(512)S(4)} %get-tuple-element.17.pairs_ref, s32[3]{0:T(128)S(4)} %get-tuple-element.18.counts_ref, bf16[9,256,128]{2,1,0:T(8,128)(2,1)S(1)} %get-tuple-element.20.q_ref, bf16[8,256,128]{2,1,0:T(8,128)(2,1)S(1)} %bitcast.8, ...), custom_call_target="tpu_custom_call" | custom-call | flops 1 | bytes 1 | tf_op jit(solution)/shard_map/attend_early/pallas_call | solution.py:320
  61.6 2.3 %collective-permute-start.3 = (bf16[8,256,128]{2,1,0:T(8,128)(2,1)S(1)}, bf16[8,256,128]{2,1,0:T(8,128)(2,1)S(1)}, u32[]{:S(2)}, u32[]{:S(2)}) collective-permute-start(bf16[8,256,128]{2,1,0:T(8,128)(2,1)S(1)} %collective-permute-done.refs_2_), channel_id=1, source_target_pairs={{0,16},{16,0},{1,17},{17,1},{2,18},{18,2},{3,19},{19,3},{4,20},{20... | collective-permute-start | bytes 1572872 | tf_op jit(solution)/shard_map/ppermute | solution.py:366
  63.9 0.0 collective-permute-done.2.refs_0_
  63.9 2.1 %collective-permute-start.4 = (bf16[8,256,128]{2,1,0:T(8,128)(2,1)S(1)}, bf16[8,256,128]{2,1,0:T(8,128)(2,1)S(1)}, u32[]{:S(2)}, u32[]{:S(2)}) collective-permute-start(bf16[8,256,128]{2,1,0:T(8,128)(2,1)S(1)} %collective-permute-done.2.refs_0_), channel_id=1, source_target_pairs={{0,16},{16,0},{1,17},{17,1},{2,18},{18,2},{3,19},{19,3},{4,20},{20... | collective-permute-start | bytes 1572872 | tf_op jit(solution)/shard_map/ppermute | solution.py:366
  66.0 0.0 collective-permute-done.5.refs_0_
  66.0 4.2 %collective-permute-start.6 = (bf16[8,256,128]{2,1,0:T(8,128)(2,1)S(1)}, bf16[8,256,128]{2,1,0:T(8,128)(2,1)S(1)}, u32[]{:S(2)}, u32[]{:S(2)}) collective-permute-start(bf16[8,256,128]{2,1,0:T(8,128)(2,1)S(1)} %collective-permute-done.5.refs_0_), channel_id=1, source_target_pairs={{0,16},{16,0},{1,17},{17,1},{2,18},{18,2},{3,19},{19,3},{4,20},{20... | collective-permute-start | bytes 1572872 | tf_op jit(solution)/shard_map/ppermute | solution.py:366
  70.2 0.0 collective-permute-done.4.refs_2_
  70.2 2.6 %attend_near.1 = (f32[9,256,128]{2,1,0:T(8,128)S(1)}, f32[9,256,128]{2,1,0:T(8,128)S(1)}) custom-call(s32[300]{0:T(512)S(4)} %get-tuple-element.17.pairs_ref, s32[3]{0:T(128)S(4)} %get-tuple-element.18.counts_ref, bf16[9,256,128]{2,1,0:T(8,128)(2,1)S(1)} %get-tuple-element.20.q_ref, ...), custom_call_target="tpu_custom_call", output_to_operand_aliasing={{0}: (3, {}), {1}: (4, {})} | custom-call | flops 2 | bytes 2 | tf_op jit(solution)/shard_map/attend_near/pallas_call | solution.py:332
  72.8 0.0 collective-permute-done.6.refs_1_
  72.8 2.5 %attend_far.1 = bf16[64,16,128]{2,1,0:T(8,128)(2,1)S(1)} custom-call(s32[300]{0:T(512)S(4)} %get-tuple-element.17.pairs_ref, s32[3]{0:T(128)S(4)} %get-tuple-element.18.counts_ref, bf16[9,256,128]{2,1,0:T(8,128)(2,1)S(1)} %get-tuple-element.20.q_ref, f32[9,256,128]{2,1,0:T(8,128)S(1)} %get-tuple-element.27.best_in, ...), custom_call_target="tpu_custom_call" | custom-call | flops 1 | bytes 1 | tf_op jit(solution)/shard_map/attend_far/pallas_call | solution.py:345
  75.3 19.0 %all_to_all.11.in_ref = bf16[64,16,128]{2,1,0:T(8,128)(2,1)S(1)} all-to-all(bf16[64,16,128]{2,1,0:T(8,128)(2,1)S(1)} %attend_far.1), channel_id=1, replica_groups={{0,1,2,3,4,5,6,7,64,65,66,67,68,69,70,71,128,129,130,131,132,133,134,13..., dimensions={0} | all-to-all | bytes 524288 | tf_op jit(solution)/shard_map/all_to_all | solution.py:379
  94.2 0.8 unpack.1
  (4 shorter events, 0.0 us)
Async XLA Ops:
  1.4 50.0 %copy-start = (s32[64,12]{0,1:T(8,128)S(1)}, s32[64,12]{0,1:T(8,128)}, u32[]{:S(2)}) copy-start(s32[64,12]{0,1:T(8,128)} %param.9) | copy-start | bytes 9220
  1.4 50.0 %copy-start.1 = (s32[64]{0:T(128)S(1)}, s32[64]{0:T(128)}, u32[]{:S(2)}) copy-start(s32[64]{0:T(128)} %order_ref.1) | copy-start | bytes 772
  39.6 14.2 %collective-permute-start = (bf16[8,256,128]{2,1,0:T(8,128)(2,1)S(1)}, bf16[8,256,128]{2,1,0:T(8,128)(2,1)S(1)}, u32[]{:S(2)}, u32[]{:S(2)}) collective-permute-start(bf16[8,256,128]{2,1,0:T(8,128)(2,1)S(1)} %bitcast.5), channel_id=1, source_target_pairs={{0,8},{16,56},{1,9},{17,57},{2,10},{18,58},{3,11},{19,59},{4,12},{... | collective-permute-start | bytes 1572872 | tf_op jit(solution)/shard_map/ppermute | solution.py:367
  44.0 13.2 %collective-permute-start.1 = (bf16[8,256,128]{2,1,0:T(8,128)(2,1)S(1)}, bf16[8,256,128]{2,1,0:T(8,128)(2,1)S(1)}, u32[]{:S(2)}, u32[]{:S(2)}) collective-permute-start(bf16[8,256,128]{2,1,0:T(8,128)(2,1)S(1)} %bitcast.6), channel_id=1, source_target_pairs={{0,16},{16,0},{1,17},{17,1},{2,18},{18,2},{3,19},{19,3},{4,20},{20... | collective-permute-start | bytes 1572872 | tf_op jit(solution)/shard_map/ppermute | solution.py:366
  48.4 15.5 %collective-permute-start.2 = (bf16[8,256,128]{2,1,0:T(8,128)(2,1)S(1)}, bf16[8,256,128]{2,1,0:T(8,128)(2,1)S(1)}, u32[]{:S(2)}, u32[]{:S(2)}) collective-permute-start(bf16[8,256,128]{2,1,0:T(8,128)(2,1)S(1)} %bitcast.7), channel_id=1, source_target_pairs={{0,56},{16,8},{1,57},{17,9},{2,58},{18,10},{3,59},{19,11},{4,60},{... | collective-permute-start | bytes 1572872 | tf_op jit(solution)/shard_map/ppermute | solution.py:371
  53.8 12.2 %collective-permute-start.5 = (bf16[8,256,128]{2,1,0:T(8,128)(2,1)S(1)}, bf16[8,256,128]{2,1,0:T(8,128)(2,1)S(1)}, u32[]{:S(2)}, u32[]{:S(2)}) collective-permute-start(bf16[8,256,128]{2,1,0:T(8,128)(2,1)S(1)} %collective-permute-done.refs_2_), channel_id=1, source_target_pairs={{0,8},{16,56},{1,9},{17,57},{2,10},{18,58},{3,11},{19,59},{4,12},{... | collective-permute-start | bytes 1572872 | tf_op jit(solution)/shard_map/ppermute | solution.py:367
  61.6 8.5 %collective-permute-start.3 = (bf16[8,256,128]{2,1,0:T(8,128)(2,1)S(1)}, bf16[8,256,128]{2,1,0:T(8,128)(2,1)S(1)}, u32[]{:S(2)}, u32[]{:S(2)}) collective-permute-start(bf16[8,256,128]{2,1,0:T(8,128)(2,1)S(1)} %collective-permute-done.refs_2_), channel_id=1, source_target_pairs={{0,16},{16,0},{1,17},{17,1},{2,18},{18,2},{3,19},{19,3},{4,20},{20... | collective-permute-start | bytes 1572872 | tf_op jit(solution)/shard_map/ppermute | solution.py:366
  63.9 6.3 %collective-permute-start.4 = (bf16[8,256,128]{2,1,0:T(8,128)(2,1)S(1)}, bf16[8,256,128]{2,1,0:T(8,128)(2,1)S(1)}, u32[]{:S(2)}, u32[]{:S(2)}) collective-permute-start(bf16[8,256,128]{2,1,0:T(8,128)(2,1)S(1)} %collective-permute-done.2.refs_0_), channel_id=1, source_target_pairs={{0,16},{16,0},{1,17},{17,1},{2,18},{18,2},{3,19},{19,3},{4,20},{20... | collective-permute-start | bytes 1572872 | tf_op jit(solution)/shard_map/ppermute | solution.py:366
  66.0 6.8 %collective-permute-start.6 = (bf16[8,256,128]{2,1,0:T(8,128)(2,1)S(1)}, bf16[8,256,128]{2,1,0:T(8,128)(2,1)S(1)}, u32[]{:S(2)}, u32[]{:S(2)}) collective-permute-start(bf16[8,256,128]{2,1,0:T(8,128)(2,1)S(1)} %collective-permute-done.5.refs_0_), channel_id=1, source_target_pairs={{0,16},{16,0},{1,17},{17,1},{2,18},{18,2},{3,19},{19,3},{4,20},{20... | collective-permute-start | bytes 1572872 | tf_op jit(solution)/shard_map/ppermute | solution.py:366

commit v4 on v3

--- a/solution.py
+++ b/solution.py
@@ -161,12 +161,11 @@
         def _(t):
             run(t * QUADS * 4, QUADS * 4)
 
-        left = quads % QUADS
-        for some in range(1, QUADS):
-
-            @pl.when(left == some)
+        for some in (2, 1):
+
+            @pl.when((quads & some) != 0)
             def _():
-                run((quads - some) * 4, some * 4)
+                run((quads & (-2 * some)) * 4, some * 4)
 
     if best_in is None:
         for block in range(NY):

time: 97 us -> 97 us (level)
  transfers between devices with their start and end apart: 7 -> 7, of which waited for: 0 -> 0; matrix products, arithmetic and copies ran while one was open for 0% -> 0% of each run, Pallas kernels for 10% -> 9%
where the time goes in v4:
time: 97 us; the launch traced here: 96.1 us
  blocking collectives  57.4 us (59%)
  starting transfers between devices  24.2 us (25%)
  Pallas kernels  14 us (14%)
    all_to_all x1, blocking collectives, local(): lax.all_to_all(packed, AXES, 0, 0, tiled=True, axis_index_groups=COLUMN_G...  38.1 us
    all_to_all x1, blocking collectives, local(): lax.all_to_all(mixed, AXES, 0, 0, tiled=True, axis_index_groups=COLUMN_GR...  19.3 us
    ppermute x4, starting transfers between devices, local(): swap = lambda t: lax.ppermute(t, AXES, SWAP_CORES)  13.5 us
    ppermute x2, starting transfers between devices, local(): onward = lambda t: lax.ppermute(t, AXES, ONWARD)  7.76 us
    pallas_call x1, Pallas kernels, attend_first(): pl.pallas_call(first_kernel, out_shape=(STATE, STATE), in_specs=[SMEM] *...  3.78 us
    pallas_call x1, Pallas kernels, attend_last(): pl.pallas_call(last_kernel, out_shape=jax.ShapeDtypeStruct((COLS, SLICE /...  3.26 us
    ppermute x1, starting transfers between devices, local(): near_twin = lax.ppermute(kv, AXES, ACROSS)  3.01 us
    pallas_call x1, Pallas kernels, attend_second(): pl.pallas_call(second_kernel, out_shape=(STATE, STATE), in_specs=[SMEM] *...  2.4 us
  transfers between devices with their start and end apart: 7, of which 0 were waited for; matrix products, arithmetic and copies ran while one was open for 0% of the time, Pallas kernels for 9%

profile of v4, /device:TPU:1, one launch (start us, length us, event | category | flops | bytes accessed | tf_op | source)
XLA Modules:
  0.0 96.1 jit_solution(9692937881219275965)
XLA Ops:
  0.0 1.4 %pack.1 = bf16[64,48,128]{2,1,0:T(8,128)(2,1)S(1)} custom-call(bf16[32,3072]{1,0:T(8,128)(2,1)} %q_hbm.1, bf16[32,3072]{1,0:T(8,128)(2,1)} %k_hbm.1, bf16[32,3072]{1,0:T(8,128)(2,1)} %v_hbm.1), custom_call_target="tpu_custom_call" | custom-call | tf_op jit(solution)/shard_map/pack/pallas_call | solution.py:260
  1.4 0.0 copy-start
  1.4 0.0 copy-start.1
  1.4 38.1 %all_to_all.10.mine_ref = bf16[64,48,128]{2,1,0:T(8,128)(2,1)S(1)} all-to-all(bf16[64,48,128]{2,1,0:T(8,128)(2,1)S(1)} %pack.1), channel_id=1, replica_groups={{0,1,2,3,4,5,6,7,64,65,66,67,68,69,70,71,128,129,130,131,132,133,134,13..., dimensions={0} | all-to-all | bytes 1572864 | tf_op jit(solution)/shard_map/all_to_all | solution.py:363
  39.6 4.4 %collective-permute-start = (bf16[8,256,128]{2,1,0:T(8,128)(2,1)S(1)}, bf16[8,256,128]{2,1,0:T(8,128)(2,1)S(1)}, u32[]{:S(2)}, u32[]{:S(2)}) collective-permute-start(bf16[8,256,128]{2,1,0:T(8,128)(2,1)S(1)} %bitcast.5), channel_id=1, source_target_pairs={{0,8},{16,56},{1,9},{17,57},{2,10},{18,58},{3,11},{19,59},{4,12},{... | collective-permute-start | bytes 1572872 | tf_op jit(solution)/shard_map/ppermute | solution.py:366
  44.0 4.3 %collective-permute-start.1 = (bf16[8,256,128]{2,1,0:T(8,128)(2,1)S(1)}, bf16[8,256,128]{2,1,0:T(8,128)(2,1)S(1)}, u32[]{:S(2)}, u32[]{:S(2)}) collective-permute-start(bf16[8,256,128]{2,1,0:T(8,128)(2,1)S(1)} %bitcast.6), channel_id=1, source_target_pairs={{0,16},{16,0},{1,17},{17,1},{2,18},{18,2},{3,19},{19,3},{4,20},{20... | collective-permute-start | bytes 1572872 | tf_op jit(solution)/shard_map/ppermute | solution.py:365
  48.3 0.1 pad_add_fusion.place_ref
  48.4 3.0 %collective-permute-start.2 = (bf16[8,256,128]{2,1,0:T(8,128)(2,1)S(1)}, bf16[8,256,128]{2,1,0:T(8,128)(2,1)S(1)}, u32[]{:S(2)}, u32[]{:S(2)}) collective-permute-start(bf16[8,256,128]{2,1,0:T(8,128)(2,1)S(1)} %bitcast.7), channel_id=1, source_target_pairs={{0,56},{16,8},{1,57},{17,9},{2,58},{18,10},{3,59},{19,11},{4,60},{... | collective-permute-start | bytes 1572872 | tf_op jit(solution)/shard_map/ppermute | solution.py:370
  51.4 2.4 %plan_pairs.1 = (bf16[9,256,128]{2,1,0:T(8,128)(2,1)S(1)}, s32[300]{0:T(512)S(4)}, s32[3]{0:T(128)S(4)}) custom-call(s32[64]{0:T(128)S(1)} %copy-done.1, s32[12,64]{1,0:T(8,128)S(1)} %bitcast.9, s32[3]{0:T(128)S(1)} %pad_add_fusion.place_ref, bf16[64,48,128]{2,1,0:T(8,128)(2,1)S(1)} %all_to_all.10.mine_ref), custom_call_target="tpu_custom_call" | custom-call | flops 1 | bytes 1 | tf_op jit(solution)/shard_map/plan_pairs/pallas_call | solution.py:303
  53.8 0.0 collective-permute-done.refs_2_
  53.8 3.4 %collective-permute-start.5 = (bf16[8,256,128]{2,1,0:T(8,128)(2,1)S(1)}, bf16[8,256,128]{2,1,0:T(8,128)(2,1)S(1)}, u32[]{:S(2)}, u32[]{:S(2)}) collective-permute-start(bf16[8,256,128]{2,1,0:T(8,128)(2,1)S(1)} %collective-permute-done.refs_2_), channel_id=1, source_target_pairs={{0,8},{16,56},{1,9},{17,57},{2,10},{18,58},{3,11},{19,59},{4,12},{... | collective-permute-start | bytes 1572872 | tf_op jit(solution)/shard_map/ppermute | solution.py:366
  57.2 0.0 collective-permute-done.1.refs_1_
  57.2 3.8 %attend_early.1 = (f32[9,256,128]{2,1,0:T(8,128)S(1)}, f32[9,256,128]{2,1,0:T(8,128)S(1)}) custom-call(s32[300]{0:T(512)S(4)} %get-tuple-element.17.pairs_ref, s32[3]{0:T(128)S(4)} %get-tuple-element.18.counts_ref, bf16[9,256,128]{2,1,0:T(8,128)(2,1)S(1)} %get-tuple-element.20.q_ref, bf16[8,256,128]{2,1,0:T(8,128)(2,1)S(1)} %bitcast.8, ...), custom_call_target="tpu_custom_call" | custom-call | flops 1 | bytes 1 | tf_op jit(solution)/shard_map/attend_early/pallas_call | solution.py:319
  61.0 2.9 %collective-permute-start.3 = (bf16[8,256,128]{2,1,0:T(8,128)(2,1)S(1)}, bf16[8,256,128]{2,1,0:T(8,128)(2,1)S(1)}, u32[]{:S(2)}, u32[]{:S(2)}) collective-permute-start(bf16[8,256,128]{2,1,0:T(8,128)(2,1)S(1)} %collective-permute-done.refs_2_), channel_id=1, source_target_pairs={{0,16},{16,0},{1,17},{17,1},{2,18},{18,2},{3,19},{19,3},{4,20},{20... | collective-permute-start | bytes 1572872 | tf_op jit(solution)/shard_map/ppermute | solution.py:365
  63.9 0.0 collective-permute-done.2.refs_0_
  63.9 1.9 %collective-permute-start.4 = (bf16[8,256,128]{2,1,0:T(8,128)(2,1)S(1)}, bf16[8,256,128]{2,1,0:T(8,128)(2,1)S(1)}, u32[]{:S(2)}, u32[]{:S(2)}) collective-permute-start(bf16[8,256,128]{2,1,0:T(8,128)(2,1)S(1)} %collective-permute-done.2.refs_0_), channel_id=1, source_target_pairs={{0,16},{16,0},{1,17},{17,1},{2,18},{18,2},{3,19},{19,3},{4,20},{20... | collective-permute-start | bytes 1572872 | tf_op jit(solution)/shard_map/ppermute | solution.py:365
  65.8 0.0 collective-permute-done.5.refs_0_
  65.8 4.3 %collective-permute-start.6 = (bf16[8,256,128]{2,1,0:T(8,128)(2,1)S(1)}, bf16[8,256,128]{2,1,0:T(8,128)(2,1)S(1)}, u32[]{:S(2)}, u32[]{:S(2)}) collective-permute-start(bf16[8,256,128]{2,1,0:T(8,128)(2,1)S(1)} %collective-permute-done.5.refs_0_), channel_id=1, source_target_pairs={{0,16},{16,0},{1,17},{17,1},{2,18},{18,2},{3,19},{19,3},{4,20},{20... | collective-permute-start | bytes 1572872 | tf_op jit(solution)/shard_map/ppermute | solution.py:365
  70.2 0.0 collective-permute-done.4.refs_2_
  70.2 2.4 %attend_near.1 = (f32[9,256,128]{2,1,0:T(8,128)S(1)}, f32[9,256,128]{2,1,0:T(8,128)S(1)}) custom-call(s32[300]{0:T(512)S(4)} %get-tuple-element.17.pairs_ref, s32[3]{0:T(128)S(4)} %get-tuple-element.18.counts_ref, bf16[9,256,128]{2,1,0:T(8,128)(2,1)S(1)} %get-tuple-element.20.q_ref, ...), custom_call_target="tpu_custom_call", output_to_operand_aliasing={{0}: (3, {}), {1}: (4, {})} | custom-call | flops 2 | bytes 2 | tf_op jit(solution)/shard_map/attend_near/pallas_call | solution.py:331
  72.6 0.0 collective-permute-done.6.refs_1_
  72.6 3.3 %attend_far.1 = bf16[64,16,128]{2,1,0:T(8,128)(2,1)S(1)} custom-call(s32[300]{0:T(512)S(4)} %get-tuple-element.17.pairs_ref, s32[3]{0:T(128)S(4)} %get-tuple-element.18.counts_ref, bf16[9,256,128]{2,1,0:T(8,128)(2,1)S(1)} %get-tuple-element.20.q_ref, f32[9,256,128]{2,1,0:T(8,128)S(1)} %get-tuple-element.27.best_in, ...), custom_call_target="tpu_custom_call" | custom-call | flops 1 | bytes 1 | tf_op jit(solution)/shard_map/attend_far/pallas_call | solution.py:344
  75.9 19.3 %all_to_all.11.in_ref = bf16[64,16,128]{2,1,0:T(8,128)(2,1)S(1)} all-to-all(bf16[64,16,128]{2,1,0:T(8,128)(2,1)S(1)} %attend_far.1), channel_id=1, replica_groups={{0,1,2,3,4,5,6,7,64,65,66,67,68,69,70,71,128,129,130,131,132,133,134,13..., dimensions={0} | all-to-all | bytes 524288 | tf_op jit(solution)/shard_map/all_to_all | solution.py:378
  95.1 0.8 unpack.1
  (4 shorter events, 0.0 us)
Async XLA Ops:
  1.4 50.0 %copy-start = (s32[64,12]{0,1:T(8,128)S(1)}, s32[64,12]{0,1:T(8,128)}, u32[]{:S(2)}) copy-start(s32[64,12]{0,1:T(8,128)} %param.9) | copy-start | bytes 9220
  1.4 50.0 %copy-start.1 = (s32[64]{0:T(128)S(1)}, s32[64]{0:T(128)}, u32[]{:S(2)}) copy-start(s32[64]{0:T(128)} %order_ref.1) | copy-start | bytes 772
  39.6 14.2 %collective-permute-start = (bf16[8,256,128]{2,1,0:T(8,128)(2,1)S(1)}, bf16[8,256,128]{2,1,0:T(8,128)(2,1)S(1)}, u32[]{:S(2)}, u32[]{:S(2)}) collective-permute-start(bf16[8,256,128]{2,1,0:T(8,128)(2,1)S(1)} %bitcast.5), channel_id=1, source_target_pairs={{0,8},{16,56},{1,9},{17,57},{2,10},{18,58},{3,11},{19,59},{4,12},{... | collective-permute-start | bytes 1572872 | tf_op jit(solution)/shard_map/ppermute | solution.py:366
  44.0 13.2 %collective-permute-start.1 = (bf16[8,256,128]{2,1,0:T(8,128)(2,1)S(1)}, bf16[8,256,128]{2,1,0:T(8,128)(2,1)S(1)}, u32[]{:S(2)}, u32[]{:S(2)}) collective-permute-start(bf16[8,256,128]{2,1,0:T(8,128)(2,1)S(1)} %bitcast.6), channel_id=1, source_target_pairs={{0,16},{16,0},{1,17},{17,1},{2,18},{18,2},{3,19},{19,3},{4,20},{20... | collective-permute-start | bytes 1572872 | tf_op jit(solution)/shard_map/ppermute | solution.py:365
  48.4 15.5 %collective-permute-start.2 = (bf16[8,256,128]{2,1,0:T(8,128)(2,1)S(1)}, bf16[8,256,128]{2,1,0:T(8,128)(2,1)S(1)}, u32[]{:S(2)}, u32[]{:S(2)}) collective-permute-start(bf16[8,256,128]{2,1,0:T(8,128)(2,1)S(1)} %bitcast.7), channel_id=1, source_target_pairs={{0,56},{16,8},{1,57},{17,9},{2,58},{18,10},{3,59},{19,11},{4,60},{... | collective-permute-start | bytes 1572872 | tf_op jit(solution)/shard_map/ppermute | solution.py:370
  53.8 12.0 %collective-permute-start.5 = (bf16[8,256,128]{2,1,0:T(8,128)(2,1)S(1)}, bf16[8,256,128]{2,1,0:T(8,128)(2,1)S(1)}, u32[]{:S(2)}, u32[]{:S(2)}) collective-permute-start(bf16[8,256,128]{2,1,0:T(8,128)(2,1)S(1)} %collective-permute-done.refs_2_), channel_id=1, source_target_pairs={{0,8},{16,56},{1,9},{17,57},{2,10},{18,58},{3,11},{19,59},{4,12},{... | collective-permute-start | bytes 1572872 | tf_op jit(solution)/shard_map/ppermute | solution.py:366
  61.0 9.2 %collective-permute-start.3 = (bf16[8,256,128]{2,1,0:T(8,128)(2,1)S(1)}, bf16[8,256,128]{2,1,0:T(8,128)(2,1)S(1)}, u32[]{:S(2)}, u32[]{:S(2)}) collective-permute-start(bf16[8,256,128]{2,1,0:T(8,128)(2,1)S(1)} %collective-permute-done.refs_2_), channel_id=1, source_target_pairs={{0,16},{16,0},{1,17},{17,1},{2,18},{18,2},{3,19},{19,3},{4,20},{20... | collective-permute-start | bytes 1572872 | tf_op jit(solution)/shard_map/ppermute | solution.py:365
  63.9 6.3 %collective-permute-start.4 = (bf16[8,256,128]{2,1,0:T(8,128)(2,1)S(1)}, bf16[8,256,128]{2,1,0:T(8,128)(2,1)S(1)}, u32[]{:S(2)}, u32[]{:S(2)}) collective-permute-start(bf16[8,256,128]{2,1,0:T(8,128)(2,1)S(1)} %collective-permute-done.2.refs_0_), channel_id=1, source_target_pairs={{0,16},{16,0},{1,17},{17,1},{2,18},{18,2},{3,19},{19,3},{4,20},{20... | collective-permute-start | bytes 1572872 | tf_op jit(solution)/shard_map/ppermute | solution.py:365
  65.8 6.8 %collective-permute-start.6 = (bf16[8,256,128]{2,1,0:T(8,128)(2,1)S(1)}, bf16[8,256,128]{2,1,0:T(8,128)(2,1)S(1)}, u32[]{:S(2)}, u32[]{:S(2)}) collective-permute-start(bf16[8,256,128]{2,1,0:T(8,128)(2,1)S(1)} %collective-permute-done.5.refs_0_), channel_id=1, source_target_pairs={{0,16},{16,0},{1,17},{17,1},{2,18},{18,2},{3,19},{19,3},{4,20},{20... | collective-permute-start | bytes 1572872 | tf_op jit(solution)/shard_map/ppermute | solution.py:365

commit v5 on v4

--- a/solution.py
+++ b/solution.py
@@ -13,7 +13,7 @@
 PAIR = 2 * HD
 COLS = 64
 SLICE = 32
-PARTS = 3
+PARTS = 2
 NY = 8
 AXES = ("tm", "head")
 MASKED = -1e30

time: 97 us -> 98.5 us (1.015)
  no operation moved by 1% of the time
where the time goes in v5:
time: 98.5 us; the launch traced here: 96.7 us
  blocking collectives  57.1 us (58%)
  starting transfers between devices  24.2 us (25%)
  Pallas kernels  14.9 us (15%)
    all_to_all x1, blocking collectives, local(): lax.all_to_all(packed, AXES, 0, 0, tiled=True, axis_index_groups=COLUMN_G...  38.1 us
    all_to_all x1, blocking collectives, local(): lax.all_to_all(mixed, AXES, 0, 0, tiled=True, axis_index_groups=COLUMN_GR...  19 us
    ppermute x4, starting transfers between devices, local(): swap = lambda t: lax.ppermute(t, AXES, SWAP_CORES)  13.5 us
    ppermute x2, starting transfers between devices, local(): onward = lambda t: lax.ppermute(t, AXES, ONWARD)  7.76 us
    pallas_call x1, Pallas kernels, attend_first(): pl.pallas_call(first_kernel, out_shape=(STATE, STATE), in_specs=[SMEM] *...  3.78 us
    pallas_call x1, Pallas kernels, attend_last(): pl.pallas_call(last_kernel, out_shape=jax.ShapeDtypeStruct((COLS, SLICE /...  3.58 us
    pallas_call x1, Pallas kernels, attend_second(): pl.pallas_call(second_kernel, out_shape=(STATE, STATE), in_specs=[SMEM] *...  3.03 us
    ppermute x1, starting transfers between devices, local(): near_twin = lax.ppermute(kv, AXES, ACROSS)  3.01 us
  transfers between devices with their start and end apart: 7, of which 0 were waited for; matrix products, arithmetic and copies ran while one was open for 0% of the time, Pallas kernels for 9%

profile of v5, /device:TPU:1, one launch (start us, length us, event | category | flops | bytes accessed | tf_op | source)
XLA Modules:
  0.0 96.7 jit_solution(11889846214638762935)
XLA Ops:
  0.0 1.4 %pack.1 = bf16[64,48,128]{2,1,0:T(8,128)(2,1)S(1)} custom-call(bf16[32,3072]{1,0:T(8,128)(2,1)} %q_hbm.1, bf16[32,3072]{1,0:T(8,128)(2,1)} %k_hbm.1, bf16[32,3072]{1,0:T(8,128)(2,1)} %v_hbm.1), custom_call_target="tpu_custom_call" | custom-call | tf_op jit(solution)/shard_map/pack/pallas_call | solution.py:260
  1.4 0.0 copy-start
  1.4 0.0 copy-start.1
  1.4 38.1 %all_to_all.10.mine_ref = bf16[64,48,128]{2,1,0:T(8,128)(2,1)S(1)} all-to-all(bf16[64,48,128]{2,1,0:T(8,128)(2,1)S(1)} %pack.1), channel_id=1, replica_groups={{0,1,2,3,4,5,6,7,64,65,66,67,68,69,70,71,128,129,130,131,132,133,134,13..., dimensions={0} | all-to-all | bytes 1572864 | tf_op jit(solution)/shard_map/all_to_all | solution.py:363
  39.5 4.4 %collective-permute-start = (bf16[8,256,128]{2,1,0:T(8,128)(2,1)S(1)}, bf16[8,256,128]{2,1,0:T(8,128)(2,1)S(1)}, u32[]{:S(2)}, u32[]{:S(2)}) collective-permute-start(bf16[8,256,128]{2,1,0:T(8,128)(2,1)S(1)} %bitcast.5), channel_id=1, source_target_pairs={{0,8},{16,56},{1,9},{17,57},{2,10},{18,58},{3,11},{19,59},{4,12},{... | collective-permute-start | bytes 1572872 | tf_op jit(solution)/shard_map/ppermute | solution.py:366
  44.0 4.3 %collective-permute-start.1 = (bf16[8,256,128]{2,1,0:T(8,128)(2,1)S(1)}, bf16[8,256,128]{2,1,0:T(8,128)(2,1)S(1)}, u32[]{:S(2)}, u32[]{:S(2)}) collective-permute-start(bf16[8,256,128]{2,1,0:T(8,128)(2,1)S(1)} %bitcast.6), channel_id=1, source_target_pairs={{0,16},{16,0},{1,17},{17,1},{2,18},{18,2},{3,19},{19,3},{4,20},{20... | collective-permute-start | bytes 1572872 | tf_op jit(solution)/shard_map/ppermute | solution.py:365
  48.3 0.1 pad_add_fusion.place_ref
  48.4 3.0 %collective-permute-start.2 = (bf16[8,256,128]{2,1,0:T(8,128)(2,1)S(1)}, bf16[8,256,128]{2,1,0:T(8,128)(2,1)S(1)}, u32[]{:S(2)}, u32[]{:S(2)}) collective-permute-start(bf16[8,256,128]{2,1,0:T(8,128)(2,1)S(1)} %bitcast.7), channel_id=1, source_target_pairs={{0,56},{16,8},{1,57},{17,9},{2,58},{18,10},{3,59},{19,11},{4,60},{... | collective-permute-start | bytes 1572872 | tf_op jit(solution)/shard_map/ppermute | solution.py:370
  51.4 2.4 %plan_pairs.1 = (bf16[9,256,128]{2,1,0:T(8,128)(2,1)S(1)}, s32[300]{0:T(512)S(4)}, s32[3]{0:T(128)S(4)}) custom-call(s32[64]{0:T(128)S(1)} %copy-done.1, s32[12,64]{1,0:T(8,128)S(1)} %bitcast.9, s32[3]{0:T(128)S(1)} %pad_add_fusion.place_ref, bf16[64,48,128]{2,1,0:T(8,128)(2,1)S(1)} %all_to_all.10.mine_ref), custom_call_target="tpu_custom_call" | custom-call | flops 1 | bytes 1 | tf_op jit(solution)/shard_map/plan_pairs/pallas_call | solution.py:303
  53.8 0.0 collective-permute-done.refs_2_
  53.8 3.4 %collective-permute-start.5 = (bf16[8,256,128]{2,1,0:T(8,128)(2,1)S(1)}, bf16[8,256,128]{2,1,0:T(8,128)(2,1)S(1)}, u32[]{:S(2)}, u32[]{:S(2)}) collective-permute-start(bf16[8,256,128]{2,1,0:T(8,128)(2,1)S(1)} %collective-permute-done.refs_2_), channel_id=1, source_target_pairs={{0,8},{16,56},{1,9},{17,57},{2,10},{18,58},{3,11},{19,59},{4,12},{... | collective-permute-start | bytes 1572872 | tf_op jit(solution)/shard_map/ppermute | solution.py:366
  57.2 0.0 collective-permute-done.1.refs_1_
  57.2 3.8 %attend_early.1 = (f32[9,256,128]{2,1,0:T(8,128)S(1)}, f32[9,256,128]{2,1,0:T(8,128)S(1)}) custom-call(s32[300]{0:T(512)S(4)} %get-tuple-element.17.pairs_ref, s32[3]{0:T(128)S(4)} %get-tuple-element.18.counts_ref, bf16[9,256,128]{2,1,0:T(8,128)(2,1)S(1)} %get-tuple-element.20.q_ref, bf16[8,256,128]{2,1,0:T(8,128)(2,1)S(1)} %bitcast.8, ...), custom_call_target="tpu_custom_call" | custom-call | flops 1 | bytes 1 | tf_op jit(solution)/shard_map/attend_early/pallas_call | solution.py:319
  61.0 2.9 %collective-permute-start.3 = (bf16[8,256,128]{2,1,0:T(8,128)(2,1)S(1)}, bf16[8,256,128]{2,1,0:T(8,128)(2,1)S(1)}, u32[]{:S(2)}, u32[]{:S(2)}) collective-permute-start(bf16[8,256,128]{2,1,0:T(8,128)(2,1)S(1)} %collective-permute-done.refs_2_), channel_id=1, source_target_pairs={{0,16},{16,0},{1,17},{17,1},{2,18},{18,2},{3,19},{19,3},{4,20},{20... | collective-permute-start | bytes 1572872 | tf_op jit(solution)/shard_map/ppermute | solution.py:365
  63.9 0.0 collective-permute-done.2.refs_0_
  63.9 1.9 %collective-permute-start.4 = (bf16[8,256,128]{2,1,0:T(8,128)(2,1)S(1)}, bf16[8,256,128]{2,1,0:T(8,128)(2,1)S(1)}, u32[]{:S(2)}, u32[]{:S(2)}) collective-permute-start(bf16[8,256,128]{2,1,0:T(8,128)(2,1)S(1)} %collective-permute-done.2.refs_0_), channel_id=1, source_target_pairs={{0,16},{16,0},{1,17},{17,1},{2,18},{18,2},{3,19},{19,3},{4,20},{20... | collective-permute-start | bytes 1572872 | tf_op jit(solution)/shard_map/ppermute | solution.py:365
  65.8 0.0 collective-permute-done.5.refs_0_
  65.8 4.3 %collective-permute-start.6 = (bf16[8,256,128]{2,1,0:T(8,128)(2,1)S(1)}, bf16[8,256,128]{2,1,0:T(8,128)(2,1)S(1)}, u32[]{:S(2)}, u32[]{:S(2)}) collective-permute-start(bf16[8,256,128]{2,1,0:T(8,128)(2,1)S(1)} %collective-permute-done.5.refs_0_), channel_id=1, source_target_pairs={{0,16},{16,0},{1,17},{17,1},{2,18},{18,2},{3,19},{19,3},{4,20},{20... | collective-permute-start | bytes 1572872 | tf_op jit(solution)/shard_map/ppermute | solution.py:365
  70.2 0.0 collective-permute-done.4.refs_2_
  70.2 3.0 %attend_near.1 = (f32[9,256,128]{2,1,0:T(8,128)S(1)}, f32[9,256,128]{2,1,0:T(8,128)S(1)}) custom-call(s32[300]{0:T(512)S(4)} %get-tuple-element.17.pairs_ref, s32[3]{0:T(128)S(4)} %get-tuple-element.18.counts_ref, bf16[9,256,128]{2,1,0:T(8,128)(2,1)S(1)} %get-tuple-element.20.q_ref, ...), custom_call_target="tpu_custom_call", output_to_operand_aliasing={{0}: (3, {}), {1}: (4, {})} | custom-call | flops 2 | bytes 2 | tf_op jit(solution)/shard_map/attend_near/pallas_call | solution.py:331
  73.2 0.0 collective-permute-done.6.refs_1_
  73.2 3.6 %attend_far.1 = bf16[64,16,128]{2,1,0:T(8,128)(2,1)S(1)} custom-call(s32[300]{0:T(512)S(4)} %get-tuple-element.17.pairs_ref, s32[3]{0:T(128)S(4)} %get-tuple-element.18.counts_ref, bf16[9,256,128]{2,1,0:T(8,128)(2,1)S(1)} %get-tuple-element.20.q_ref, f32[9,256,128]{2,1,0:T(8,128)S(1)} %get-tuple-element.27.best_in, ...), custom_call_target="tpu_custom_call" | custom-call | flops 1 | bytes 1 | tf_op jit(solution)/shard_map/attend_far/pallas_call | solution.py:344
  76.8 19.0 %all_to_all.11.in_ref = bf16[64,16,128]{2,1,0:T(8,128)(2,1)S(1)} all-to-all(bf16[64,16,128]{2,1,0:T(8,128)(2,1)S(1)} %attend_far.1), channel_id=1, replica_groups={{0,1,2,3,4,5,6,7,64,65,66,67,68,69,70,71,128,129,130,131,132,133,134,13..., dimensions={0} | all-to-all | bytes 524288 | tf_op jit(solution)/shard_map/all_to_all | solution.py:378
  95.8 0.8 unpack.1
  (4 shorter events, 0.0 us)
Async XLA Ops:
  1.4 50.0 %copy-start = (s32[64,12]{0,1:T(8,128)S(1)}, s32[64,12]{0,1:T(8,128)}, u32[]{:S(2)}) copy-start(s32[64,12]{0,1:T(8,128)} %param.9) | copy-start | bytes 9220
  1.4 50.0 %copy-start.1 = (s32[64]{0:T(128)S(1)}, s32[64]{0:T(128)}, u32[]{:S(2)}) copy-start(s32[64]{0:T(128)} %order_ref.1) | copy-start | bytes 772
  39.5 14.2 %collective-permute-start = (bf16[8,256,128]{2,1,0:T(8,128)(2,1)S(1)}, bf16[8,256,128]{2,1,0:T(8,128)(2,1)S(1)}, u32[]{:S(2)}, u32[]{:S(2)}) collective-permute-start(bf16[8,256,128]{2,1,0:T(8,128)(2,1)S(1)} %bitcast.5), channel_id=1, source_target_pairs={{0,8},{16,56},{1,9},{17,57},{2,10},{18,58},{3,11},{19,59},{4,12},{... | collective-permute-start | bytes 1572872 | tf_op jit(solution)/shard_map/ppermute | solution.py:366
  44.0 13.2 %collective-permute-start.1 = (bf16[8,256,128]{2,1,0:T(8,128)(2,1)S(1)}, bf16[8,256,128]{2,1,0:T(8,128)(2,1)S(1)}, u32[]{:S(2)}, u32[]{:S(2)}) collective-permute-start(bf16[8,256,128]{2,1,0:T(8,128)(2,1)S(1)} %bitcast.6), channel_id=1, source_target_pairs={{0,16},{16,0},{1,17},{17,1},{2,18},{18,2},{3,19},{19,3},{4,20},{20... | collective-permute-start | bytes 1572872 | tf_op jit(solution)/shard_map/ppermute | solution.py:365
  48.4 15.5 %collective-permute-start.2 = (bf16[8,256,128]{2,1,0:T(8,128)(2,1)S(1)}, bf16[8,256,128]{2,1,0:T(8,128)(2,1)S(1)}, u32[]{:S(2)}, u32[]{:S(2)}) collective-permute-start(bf16[8,256,128]{2,1,0:T(8,128)(2,1)S(1)} %bitcast.7), channel_id=1, source_target_pairs={{0,56},{16,8},{1,57},{17,9},{2,58},{18,10},{3,59},{19,11},{4,60},{... | collective-permute-start | bytes 1572872 | tf_op jit(solution)/shard_map/ppermute | solution.py:370
  53.8 12.0 %collective-permute-start.5 = (bf16[8,256,128]{2,1,0:T(8,128)(2,1)S(1)}, bf16[8,256,128]{2,1,0:T(8,128)(2,1)S(1)}, u32[]{:S(2)}, u32[]{:S(2)}) collective-permute-start(bf16[8,256,128]{2,1,0:T(8,128)(2,1)S(1)} %collective-permute-done.refs_2_), channel_id=1, source_target_pairs={{0,8},{16,56},{1,9},{17,57},{2,10},{18,58},{3,11},{19,59},{4,12},{... | collective-permute-start | bytes 1572872 | tf_op jit(solution)/shard_map/ppermute | solution.py:366
  61.0 9.2 %collective-permute-start.3 = (bf16[8,256,128]{2,1,0:T(8,128)(2,1)S(1)}, bf16[8,256,128]{2,1,0:T(8,128)(2,1)S(1)}, u32[]{:S(2)}, u32[]{:S(2)}) collective-permute-start(bf16[8,256,128]{2,1,0:T(8,128)(2,1)S(1)} %collective-permute-done.refs_2_), channel_id=1, source_target_pairs={{0,16},{16,0},{1,17},{17,1},{2,18},{18,2},{3,19},{19,3},{4,20},{20... | collective-permute-start | bytes 1572872 | tf_op jit(solution)/shard_map/ppermute | solution.py:365
  63.9 6.3 %collective-permute-start.4 = (bf16[8,256,128]{2,1,0:T(8,128)(2,1)S(1)}, bf16[8,256,128]{2,1,0:T(8,128)(2,1)S(1)}, u32[]{:S(2)}, u32[]{:S(2)}) collective-permute-start(bf16[8,256,128]{2,1,0:T(8,128)(2,1)S(1)} %collective-permute-done.2.refs_0_), channel_id=1, source_target_pairs={{0,16},{16,0},{1,17},{17,1},{2,18},{18,2},{3,19},{19,3},{4,20},{20... | collective-permute-start | bytes 1572872 | tf_op jit(solution)/shard_map/ppermute | solution.py:365
  65.8 7.4 %collective-permute-start.6 = (bf16[8,256,128]{2,1,0:T(8,128)(2,1)S(1)}, bf16[8,256,128]{2,1,0:T(8,128)(2,1)S(1)}, u32[]{:S(2)}, u32[]{:S(2)}) collective-permute-start(bf16[8,256,128]{2,1,0:T(8,128)(2,1)S(1)} %collective-permute-done.5.refs_0_), channel_id=1, source_target_pairs={{0,16},{16,0},{1,17},{17,1},{2,18},{18,2},{3,19},{19,3},{4,20},{20... | collective-permute-start | bytes 1572872 | tf_op jit(solution)/shard_map/ppermute | solution.py:365
